TPU v7x, 32 devices: a whole 2x2x4 slice. The times are simulated.
32 devices in a mesh: dp: 4 (over y, x), seq: 8 (over z, core).
Axes of the slice: x: 2, y: 2, z: 4, core: 2. Of those that a mesh axis runs over, the one named last changes fastest.
Arguments:
- queries: bfloat16 [4, 1024, 512], P('dp', 'seq'), may hold values from -6 to 6
- keys: bfloat16 [4, 1024, 512], P('dp', 'seq'), may hold values from -6 to 6
- values: bfloat16 [4, 1024, 512], P('dp', 'seq'), may hold values from -6 to 6
- gates: bfloat16 [4, 1024, 512], P('dp', 'seq'), may hold values from -6 to 6
- lengths: int32 [4], P('dp'), may hold values from 256 to 1024, as said below
- rab_steps: float32 [4, 16], replicated, may hold values from -3 to 3
- out_grad: bfloat16 [4, 1024, 512], P('dp', 'seq'), may hold values from -6 to 6
Outputs:
- gated: bfloat16 [4, 1024, 512], P('dp', 'seq')
- query_grad: bfloat16 [4, 1024, 512], P('dp', 'seq')
- key_grad: bfloat16 [4, 1024, 512], P('dp', 'seq')
- value_grad: bfloat16 [4, 1024, 512], P('dp', 'seq')
- gate_grad: bfloat16 [4, 1024, 512], P('dp', 'seq')
- rab_grad: float32 [4, 16], replicated
Inputs may be any that keep to these rules, and one draw needn't show every extreme that they name: Events at and after position lengths[u] of user u are padding; some user fills all 1024 slots.
All inputs are finite; a program needn't handle non-finite values.
Results may differ from a plain program's by a relative error of at most 0.0057.
Values may be sent and summed in bfloat16 or wider, within the bound.
No kernel may reach another device: no remote copies, remote signals or barrier semaphores. Data moves between devices by JAX's collectives and lax.ppermute only.
A program may use at most 64 MiB of HBM per device.

v0:
```python
import jax
import jax.numpy as jnp
from jax import lax
from jax.sharding import PartitionSpec as P


def split_heads(rows_in, head_count):
    return rows_in.reshape(rows_in.shape[0], head_count, rows_in.shape[1] // head_count)


def band_layout(query_pos, key_pos, band_width, bucket_count):
    offset = query_pos[:, None] - key_pos[None, :]
    lowest = query_pos[0] - key_pos[-1]
    base_band = jnp.clip(jnp.floor_divide(lowest, band_width), 0, bucket_count - 1)
    span = query_pos.shape[0] + key_pos.shape[0] - 1
    crossings = min(bucket_count, max(0, -(-(span - 1) // band_width)))
    return (offset, base_band, crossings)


def pair_terms(
    query_rows,
    key_rows,
    value_rows,
    dgrad_rows,
    query_pos,
    key_pos,
    rab_steps,
    valid_len,
    band_width,
    inv_root,
    attn_scale,
):
    head_count = rab_steps.shape[0]
    bucket_count = rab_steps.shape[1]
    raw_score = (
        jnp.einsum(
            "ihd,jhd->hij",
            split_heads(query_rows, head_count),
            split_heads(key_rows, head_count),
            preferred_element_type=jnp.float32,
        )
        * inv_root
    )
    offset, base_band, crossings = band_layout(query_pos, key_pos, band_width, bucket_count)
    live_mask = (offset >= 0) & (query_pos[:, None] < valid_len) & (key_pos[None, :] < valid_len)
    cumulative = jnp.cumsum(rab_steps, axis=1)
    base_bias = lax.dynamic_slice_in_dim(cumulative, base_band, 1, 1)
    bias_sum = jnp.broadcast_to(base_bias[:, :, None], raw_score.shape)
    for step_index in range(1, crossings + 1):
        level = base_band + step_index
        inside = (level < bucket_count).astype(jnp.float32)
        step_value = (
            lax.dynamic_slice_in_dim(rab_steps, jnp.minimum(level, bucket_count - 1), 1, 1) * inside
        )
        ramp_mask = (offset >= level * band_width).astype(jnp.float32)
        bias_sum = bias_sum + step_value[:, :, None] * ramp_mask[None]
    pre_act = raw_score + bias_sum
    sigmoid_pre = jax.nn.sigmoid(pre_act)
    weight = jnp.where(live_mask[None], pre_act * sigmoid_pre * attn_scale, 0.0)
    dweight = jnp.einsum(
        "ihd,jhd->hij",
        split_heads(dgrad_rows, head_count),
        split_heads(value_rows, head_count),
        preferred_element_type=jnp.float32,
    )
    dpre = jnp.where(
        live_mask[None],
        dweight * attn_scale * sigmoid_pre * (1.0 + pre_act * (1.0 - sigmoid_pre)),
        0.0,
    )
    return (weight, dpre, (offset, base_band, crossings))


def band_sums(dpre, layout, band_width, bucket_count):
    offset, base_band, crossings = layout
    band_index = jnp.arange(bucket_count, dtype=jnp.int32)[None, :]
    whole = jnp.sum(dpre, axis=(1, 2))
    result = jnp.where(band_index <= base_band, whole[:, None], 0.0)
    for step_index in range(1, crossings + 1):
        level = base_band + step_index
        ramp_mask = (offset >= level * band_width).astype(jnp.float32)
        suffix = jnp.sum(dpre * ramp_mask[None], axis=(1, 2))
        result = result + jnp.where(band_index == level, suffix[:, None], 0.0)
    return result


def in_blocks(step_fn, carry, pieces, start, row_count):
    total_rows = pieces[0].shape[0]
    limit = max(8, 65536 // row_count)
    sub_rows = 1
    for divisor in range(1, total_rows + 1):
        if total_rows % divisor == 0 and divisor <= limit:
            sub_rows = divisor
    if sub_rows == total_rows:
        return step_fn(carry, pieces[0], pieces[1], start)

    def inner(held, index):
        begin = (index * sub_rows).astype(jnp.int32)
        first_part = lax.dynamic_slice_in_dim(pieces[0], begin, sub_rows, 0)
        second_part = lax.dynamic_slice_in_dim(pieces[1], begin, sub_rows, 0)
        return (step_fn(held, first_part, second_part, start + begin), None)

    result, unused = lax.scan(inner, carry, jnp.arange(total_rows // sub_rows, dtype=jnp.int32))
    return result


def body(queries, keys, values, gates, lengths, rab_steps, out_grad):
    row_count = queries.shape[1]
    feat_width = queries.shape[2]
    head_count = rab_steps.shape[0]
    bucket_count = rab_steps.shape[1]
    total_len = row_count * lax.axis_size("seq")
    band_width = total_len // bucket_count
    inv_root = (feat_width // head_count) ** (-0.5)
    attn_scale = total_len ** (-0.5)
    first_row = lax.axis_index("seq") * row_count
    valid_len = lengths[0]
    own_query = queries[0]
    own_key = keys[0]
    own_value = values[0]
    own_gate = gates[0]
    own_outgrad = out_grad[0]
    dgrad = (own_outgrad.astype(jnp.float32) * own_gate.astype(jnp.float32)).astype(jnp.bfloat16)
    own_pos = first_row + jnp.arange(row_count, dtype=jnp.int32)

    def query_side(carry, key_piece, value_piece, start):
        attended, query_acc, rab_acc = carry
        key_pos = start + jnp.arange(key_piece.shape[0], dtype=jnp.int32)
        weight, dpre, layout = pair_terms(
            own_query,
            key_piece,
            value_piece,
            dgrad,
            own_pos,
            key_pos,
            rab_steps,
            valid_len,
            band_width,
            inv_root,
            attn_scale,
        )
        attended_new = jnp.einsum(
            "hij,jhd->ihd",
            weight.astype(jnp.bfloat16),
            split_heads(value_piece, head_count),
            preferred_element_type=jnp.float32,
        ).reshape(row_count, feat_width)
        query_new = (
            jnp.einsum(
                "hij,jhd->ihd",
                dpre.astype(jnp.bfloat16),
                split_heads(key_piece, head_count),
                preferred_element_type=jnp.float32,
            ).reshape(row_count, feat_width)
            * inv_root
        )
        return (
            attended + attended_new,
            query_acc + query_new,
            rab_acc + band_sums(dpre, layout, band_width, bucket_count),
        )

    def key_side(carry, query_piece, dgrad_piece, start):
        key_acc, value_acc = carry
        query_pos = start + jnp.arange(query_piece.shape[0], dtype=jnp.int32)
        weight, dpre, layout = pair_terms(
            query_piece,
            own_key,
            own_value,
            dgrad_piece,
            query_pos,
            own_pos,
            rab_steps,
            valid_len,
            band_width,
            inv_root,
            attn_scale,
        )
        value_new = jnp.einsum(
            "hij,ihd->jhd",
            weight.astype(jnp.bfloat16),
            split_heads(dgrad_piece, head_count),
            preferred_element_type=jnp.float32,
        ).reshape(row_count, feat_width)
        key_new = (
            jnp.einsum(
                "hij,ihd->jhd",
                dpre.astype(jnp.bfloat16),
                split_heads(query_piece, head_count),
                preferred_element_type=jnp.float32,
            ).reshape(row_count, feat_width)
            * inv_root
        )
        return (key_acc + key_new, value_acc + value_new)

    def query_step(carry, key_piece, value_piece, start):
        nothing_live = (
            (start >= first_row + row_count) | (start >= valid_len) | (first_row >= valid_len)
        )
        return lax.cond(
            nothing_live,
            lambda held: held,
            lambda held: query_side(held, key_piece, value_piece, start),
            carry,
        )

    def key_step(carry, query_piece, dgrad_piece, start):
        nothing_live = (
            (start + query_piece.shape[0] <= first_row)
            | (start >= valid_len)
            | (first_row >= valid_len)
        )
        return lax.cond(
            nothing_live,
            lambda held: held,
            lambda held: key_side(held, query_piece, dgrad_piece, start),
            carry,
        )

    zero_rows = jnp.zeros((row_count, feat_width), jnp.float32)
    zero_bias = jnp.zeros((head_count, bucket_count), jnp.float32)
    attended, query_acc, rab_acc = in_blocks(
        query_step,
        (zero_rows, zero_rows, zero_bias),
        (
            lax.all_gather(own_key, "seq", axis=0, tiled=True),
            lax.all_gather(own_value, "seq", axis=0, tiled=True),
        ),
        jnp.int32(0),
        row_count,
    )
    key_acc, value_acc = in_blocks(
        key_step,
        (zero_rows, zero_rows),
        (
            lax.all_gather(own_query, "seq", axis=0, tiled=True),
            lax.all_gather(dgrad, "seq", axis=0, tiled=True),
        ),
        jnp.int32(0),
        row_count,
    )
    rab_grad = lax.psum(rab_acc, ("dp", "seq")) / total_len
    gated = (attended * own_gate.astype(jnp.float32)).astype(jnp.bfloat16)
    gate_grad = (own_outgrad.astype(jnp.float32) * attended).astype(jnp.bfloat16)
    return (
        gated[None],
        query_acc.astype(jnp.bfloat16)[None],
        key_acc.astype(jnp.bfloat16)[None],
        value_acc.astype(jnp.bfloat16)[None],
        gate_grad[None],
        rab_grad,
    )


def solution(mesh):
    placed = (
        P("dp", "seq", None),
        P("dp", "seq", None),
        P("dp", "seq", None),
        P("dp", "seq", None),
        P("dp"),
        P(),
        P("dp", "seq", None),
    )
    return jax.shard_map(
        body,
        mesh=mesh,
        in_specs=placed,
        out_specs=(
            P("dp", "seq", None),
            P("dp", "seq", None),
            P("dp", "seq", None),
            P("dp", "seq", None),
            P("dp", "seq", None),
            P(),
        ),
        check_vma=False,
    )
```

profile of v0, /device:TPU:0, one launch (start us, length us, event | category | flops | bytes accessed | tf_op | source)
XLA Modules:
  0.0 190.4 jit_solution(16449091001883308251)
XLA Ops:
  7.2 1.7 copy.87
  9.0 0.8 copy-done.4
  12.2 0.8 copy-done.2
  15.3 21.6 %all-gather.10.cloned.1.call-done = bf16[1,1024,512]{1,2,0:T(8,128)(2,1)} async-done(((bf16[1,128,512]{1,2,0:T(8,128)(2,1)}), bf16[1,1024,512]{1,2,0:T(8,128)(2,1)}) %all-gather.10.cloned.1.call-update) | async-done | bytes 1048592 | tf_op jit(solution)/shard_map/all_gather | solution.py:226
  36.9 24.8 %all-gather.12.cloned.1.call-done = bf16[1,1024,512]{1,2,0:T(8,128)(2,1)} async-done(((bf16[1,128,512]{1,2,0:T(8,128)(2,1)}), bf16[1,1024,512]{1,2,0:T(8,128)(2,1)}) %all-gather.12.cloned.1.call-update) | async-done | bytes 1048592 | tf_op jit(solution)/shard_map/all_gather | solution.py:227
  61.7 20.2 %while.32 = (s32[]{:T(128)}, f32[128,512]{0,1:T(8,128)S(1)}, f32[128,512]{0,1:T(8,128)S(1)}, f32[4,16]{1,0:T(4,128)S(1)}, s32[2]{0:T(128)S(1)}, /*index=5*/s32[]...) while((s32[]{:T(128)}, f32[128,512]{0,1:T(8,128)S(1)}, ...), condition=%wide.region_15.16_spmd.clone, body=%wide.region_0.15_spmd.clone.sunk | while | flops 286200192 | bytes 25112332 | solution.py:103
  64.2 13.8 %conditional.7 = ((f32[128,512]{0,1:T(8,128)S(1)}, f32[128,512]{0,1:T(8,128)S(1)}, f32[4,16]{1,0:T(4,128)S(1)})) conditional(s32[]{:T(128)} %convert_element_type.453, (s32[]{:T(128)}, s32[]{:T(128)}, s32[]{:T(128)}, bf16[1024,512]{0,1:T(8,128)(2,1)}, bf16[1,128,512]{2,1,0:T(8,128)(2,1)S(1)}, /*index=5*/f32[4,16]{0,1:T(8,128)S(1)}, ...), branch_computations={%region_1.13_spmd, %region_14.14_spmd} | conditional | flops 286200192 | bytes 25111380 | solution.py:200
  67.6 1.1 fusion.13
  70.1 1.4 constant_dynamic-slice_fusion.12
  72.2 2.1 %fusion.9 = f32[4,128,512]{1,2,0:T(8,128)S(1)} fusion(bf16[512,4,128]{0,2,1:T(8,128)(2,1)S(1)} %bitcast.125, f32[128,512]{0,1:T(8,128)} %get-tuple-element.857, f32[4]{0:T(128)} %get-tuple-element.839, f32[128,512]{0,1:T(8,128)S(1)} %get-tuple-element.848, f32[4]{0:T(128)} %get-tuple-element.840, f32[128,512]{0,1:T(8,128)S(1)} %get-tuple-element.849, ...), kind=kOutput, calls=%fused_computation.20 | convolution fusion | flops 72876032 | bytes 4325552 | tf_op jit(solution)/shard_map/while/body/eval_jaxpr/cond/branch_0_fun/ihd,jhd->hij/dot_general | solution.py:36
  75.3 1.7 fusion.113
  82.8 1.6 all-gather.8.cloned.1.call-done
  84.4 1.5 copy.93
  85.9 51.2 %psum.7 = f32[4,16]{1,0:T(4,128)S(1)} all-reduce(f32[4,16]{1,0:T(4,128)S(1)} %get-tuple-element.543), channel_id=1, replica_groups=mesh['dp'=4,'seq'=8] {'dp','seq'}, use_global_device_ids=true, to_apply=%region_21.22 | all-reduce | flops 64 | bytes 512 | tf_op jit(solution)/shard_map/psum | solution.py:242
  138.4 0.9 copy-done.3
  139.3 43.1 %while.33 = (s32[]{:T(128)}, f32[128,512]{0,1:T(8,128)S(1)}, f32[128,512]{0,1:T(8,128)S(1)}, s32[2]{0:T(128)S(1)}, s32[]{:T(128)}, /*index=5*/s32[]{:T(128)}, pr...) while((s32[]{:T(128)}, f32[128,512]{0,1:T(8,128)S(1)}, ...), condition=%wide.region_20.21_spmd.clone.clone, body=%wide.region_16.20_spmd.clone.clone.sunk | while | flops 280693568 | bytes 16460254 | solution.py:103
  141.8 18.4 %conditional.8 = ((f32[128,512]{0,1:T(8,128)S(1)}, f32[128,512]{0,1:T(8,128)S(1)})) conditional(s32[]{:T(128)} %convert_element_type.454, (s32[]{:T(128)}, s32[]{:T(128)}, s32[]{:T(128)}, bf16[1024,512]{0,1:T(8,128)(2,1)S(1)}, bf16[1,128,512]{2,1,0:T(8,128)(2,1)}, /*index=5*/bf16[1024,512]{0,1:T(8,128)(2,1)}, bf16[1,128,512]{2,1,0:T(8,128)(2,1)S(1)}, ...), branch_computations={%region_17.18_spmd, %region_19.19_spmd} | conditional | flops 280693568 | bytes 16459312 | solution.py:213
  146.3 1.4 fusion.67
  148.4 0.8 fusion.81
  149.2 1.4 constant_dynamic-slice_fusion.24
  151.3 3.4 %fusion.51 = f32[4,512,128]{2,1,0:T(8,128)} fusion(bf16[512,4,128]{0,2,1:T(8,128)(2,1)S(1)} %bitcast.129, f32[512,128]{1,0:T(8,128)} %get-tuple-element.835, f32[4]{0:T(128)S(1)} %get-tuple-element.817, f32[512,128]{1,0:T(8,128)S(1)} %get-tuple-element.826, f32[4]{0:T(128)} %get-tuple-element.818, f32[512,128]{1,0:T(8,128)S(1)} %get-tuple-element.827, ...), kind=kOutput, calls=%fused_computation.118 | convolution fusion | flops 72876032 | bytes 4325552 | tf_op jit(solution)/shard_map/while/body/eval_jaxpr/cond/branch_0_fun/ihd,jhd->hij/dot_general | solution.py:36
  155.6 0.8 copy-done.7
  156.4 2.0 %fusion.57 = f32[4,128,128]{1,2,0:T(8,128)S(1)} fusion(bf16[512,4,128]{0,2,1:T(8,128)(2,1)S(1)} %bitcast.130, bf16[512,4,128]{0,2,1:T(8,128)(2,1)S(1)} %bitcast.131, f32[4,512,128]{2,1,0:T(8,128)} %fusion.51, pred[512,128]{1,0:T(8,128)(4,1)S(1)} %copy-done.7, bf16[128,4,128]{2,1,0:T(4,128)(2,1)S(1)} %reshape_squeeze.16), kind=kOutput, calls=%fused_computation.125 | convolution fusion | flops 137166848 | bytes 2555904 | tf_op jit(solution)/shard_map/while/body/eval_jaxpr/cond/branch_0_fun/hij,ihd->jhd/dot_general | solution.py:186
  158.4 1.7 fusion.65
  163.4 18.3 %conditional.8 = ((f32[128,512]{0,1:T(8,128)S(1)}, f32[128,512]{0,1:T(8,128)S(1)})) conditional(s32[]{:T(128)} %convert_element_type.454, (s32[]{:T(128)}, s32[]{:T(128)}, s32[]{:T(128)}, bf16[1024,512]{0,1:T(8,128)(2,1)S(1)}, bf16[1,128,512]{2,1,0:T(8,128)(2,1)}, /*index=5*/bf16[1024,512]{0,1:T(8,128)(2,1)}, bf16[1,128,512]{2,1,0:T(8,128)(2,1)S(1)}, ...), branch_computations={%region_17.18_spmd, %region_19.19_spmd} | conditional | flops 280693568 | bytes 16459312 | solution.py:213
  167.8 1.4 fusion.67
  170.0 0.8 fusion.81
  170.8 1.3 constant_dynamic-slice_fusion.24
  172.8 3.4 %fusion.51 = f32[4,512,128]{2,1,0:T(8,128)} fusion(bf16[512,4,128]{0,2,1:T(8,128)(2,1)S(1)} %bitcast.129, f32[512,128]{1,0:T(8,128)} %get-tuple-element.835, f32[4]{0:T(128)S(1)} %get-tuple-element.817, f32[512,128]{1,0:T(8,128)S(1)} %get-tuple-element.826, f32[4]{0:T(128)} %get-tuple-element.818, f32[512,128]{1,0:T(8,128)S(1)} %get-tuple-element.827, ...), kind=kOutput, calls=%fused_computation.118 | convolution fusion | flops 72876032 | bytes 4325552 | tf_op jit(solution)/shard_map/while/body/eval_jaxpr/cond/branch_0_fun/ihd,jhd->hij/dot_general | solution.py:36
  177.1 0.8 copy-done.7
  177.9 2.0 %fusion.57 = f32[4,128,128]{1,2,0:T(8,128)S(1)} fusion(bf16[512,4,128]{0,2,1:T(8,128)(2,1)S(1)} %bitcast.130, bf16[512,4,128]{0,2,1:T(8,128)(2,1)S(1)} %bitcast.131, f32[4,512,128]{2,1,0:T(8,128)} %fusion.51, pred[512,128]{1,0:T(8,128)(4,1)S(1)} %copy-done.7, bf16[128,4,128]{2,1,0:T(4,128)(2,1)S(1)} %reshape_squeeze.16), kind=kOutput, calls=%fused_computation.125 | convolution fusion | flops 137166848 | bytes 2555904 | tf_op jit(solution)/shard_map/while/body/eval_jaxpr/cond/branch_0_fun/hij,ihd->jhd/dot_general | solution.py:186
  179.9 1.7 fusion.65
  (125 shorter events, 33.0 us)
Async XLA Ops:
  7.2 29.7 %all-gather.10.cloned.1.call-start = ((), (), s32[]{:S(2)}) async-start(), calls=%async_computation.1 | async-start | bytes 1179648 | tf_op jit(solution)/shard_map/all_gather | solution.py:226
  8.9 0.9 copy-start.4
  8.9 52.7 %all-gather.12.cloned.1.call-start = ((), (), s32[]{:S(2)}) async-start(), calls=%async_computation.2 | async-start | bytes 1179648 | tf_op jit(solution)/shard_map/all_gather | solution.py:227
  9.8 0.9 copy-start.11
  10.5 0.9 copy-start.9
  10.6 73.8 %all-gather.8.cloned.1.call-start = ((), (), s32[]{:S(2)}) async-start(), calls=%async_computation | async-start | bytes 1179648 | tf_op jit(solution)/shard_map/all_gather | solution.py:237
  12.2 0.9 copy-start.2
  12.2 126.2 %all-gather.14.cloned.1.call-start = ((), (), s32[]{:S(2)}) async-start(), calls=%async_computation.3 | async-start | bytes 1179648 | tf_op jit(solution)/shard_map/all_gather | solution.py:236
  14.5 0.7 copy-start.13
  61.7 0.6 copy-start.14
  72.2 2.1 %copy-start.1 = (bf16[1024,512]{0,1:T(8,128)(2,1)S(1)}, bf16[1024,512]{0,1:T(8,128)(2,1)}, u32[]{:S(2)}) copy-start(bf16[1024,512]{0,1:T(8,128)(2,1)} %get-tuple-element.480) | copy-start | bytes 3145732 | tf_op jit(solution)/shard_map/while/body/eval_jaxpr/cond
  74.3 1.0 copy-start
  74.3 0.9 copy-start.6
  74.3 1.0 copy-start.8
  78.1 0.7 copy-start.15
  78.7 0.6 copy-start.14
  81.2 0.7 copy-start.15
  82.8 54.8 %copy-start.10 = (bf16[1,128,512]{2,1,0:T(8,128)(2,1)S(1)}, bf16[1,128,512]{2,1,0:T(8,128)(2,1)}, u32[]{:S(2)}) copy-start(bf16[1,128,512]{2,1,0:T(8,128)(2,1)} %param.18) | copy-start | bytes 393220
  82.8 54.8 %copy-start.12 = (bf16[1,128,512]{2,1,0:T(8,128)(2,1)S(1)}, bf16[1,128,512]{2,1,0:T(8,128)(2,1)}, u32[]{:S(2)}) copy-start(bf16[1,128,512]{2,1,0:T(8,128)(2,1)} %param.21) | copy-start | bytes 393220
  138.4 0.9 copy-start.3
  139.3 0.6 copy-start.16
  154.6 0.9 copy-start.5
  155.5 0.8 copy-start.7
  160.2 0.7 copy-start.17
  160.9 0.6 copy-start.16
  176.1 0.9 copy-start.5
  177.1 0.8 copy-start.7
  181.7 0.7 copy-start.17
Sparse Core Ops, SparseCore 0:
  10.2 26.6 all-gather.9
  39.0 22.5 all-gather.11
  63.8 20.5 all-gather.7
  85.8 23.8 all-gather.13
where the time goes:
time: 191 us; the launch traced here: 190 us
  blocking collectives  51.2 us (27%)
  waiting for transfers between devices  48.1 us (25%)
  local copies, waits for them, and re-layouts  34.4 us (18%)
  matrix products  18.6 us (10%)
  between operations  14.5 us (8%)
  other arithmetic  14.3 us (7%)
  loops' own time  9.25 us (5%)
    psum x1, blocking collectives, body(): rab_grad = lax.psum(rab_acc, ('dp', 'seq')) / total_len  51.2 us
    all_gather x1, waiting for transfers between devices, body(): lax.all_gather(own_value, 'seq', axis=0, tiled=True)  24.8 us
    all_gather x1, waiting for transfers between devices, body(): lax.all_gather(own_key, 'seq', axis=0, tiled=True)  21.6 us
    dot_general x3, matrix products, pair_terms(): jnp.einsum('ihd,jhd->hij', split_heads(query_rows, head_count), split_hea...  8.81 us
    unnamed x21, local copies, waits for them, and re-layouts  8.8 us
    another operation x2, loops' own time, in_blocks(): lax.scan(inner, carry, jnp.arange(total_rows // sub_rows, dtype=jnp.int32))  5.4 us
    while x16, local copies, waits for them, and re-layouts  4.94 us
    dynamic_slice x3, local copies, waits for them, and re-layouts, inner(): first_part = lax.dynamic_slice_in_dim(pieces[0], begin, sub_rows, 0)  4.02 us
  transfers between devices with their start and end apart: 4, of which 3 were waited for; matrix products, arithmetic and copies ran while one was open for 10% of the time, Pallas kernels for 0%

commit v1 on v0

v1 whole, which is shorter than its diff:
```python
import functools

import jax
import jax.numpy as jnp
from jax import lax
from jax.experimental import pallas as pl
from jax.experimental.pallas import tpu as pltpu
from jax.sharding import PartitionSpec as P

F32 = jnp.float32
BF16 = jnp.bfloat16
VMEM = pl.BlockSpec(memory_space=pltpu.VMEM)
SMEM = pl.BlockSpec(memory_space=pltpu.SMEM)
HBM = pl.BlockSpec(memory_space=pltpu.HBM)
ANY = pl.BlockSpec(memory_space=pl.ANY)
VMEM_LIMIT = 40 * 1024 * 1024
PREP_LIMIT = 60 * 1024 * 1024


def nt_dot(left, right):
    return lax.dot_general(left, right, (((1,), (1,)), ((), ())), preferred_element_type=F32)


def prep_kernel(
    len_ref, q_ref, k_ref, v_ref, u_ref, og_ref,
    kv_same, kv_cross, qd_same, qd_cross, far_same, far_cross, near_ref,
    buf, copied,
    *, chips,
):
    copies = [
        pltpu.make_async_copy(source.at[0], buf.at[n], copied.at[n])
        for n, source in enumerate((k_ref, v_ref, q_ref, og_ref, u_ref))
    ]
    for copy in copies:
        copy.start()
    index = lax.axis_index("seq")
    chip, core = index // 2, lax.rem(index, 2)
    rows, width = buf.shape[1:]
    wide = width // 2
    live = index * rows + lax.broadcasted_iota(jnp.int32, (rows, 1), 0) < len_ref[0]
    for copy in copies:
        copy.wait()

    def lay_out(same, cross):
        near_ref[5] = buf[3, :, cross]
        near_ref[4] = buf[4, :, cross]
        grad = buf[3].astype(F32) * buf[4].astype(F32)
        buf[3] = jnp.where(live, grad, 0.0).astype(BF16)
        for n in range(2):
            kv_same[n] = buf[n, :, same]
            kv_cross[n] = buf[n, :, cross]
            near_ref[n] = buf[n, :, cross]
            qd_same[n] = buf[n + 2, :, same]
            qd_cross[n] = buf[n + 2, :, cross]
            near_ref[n + 2] = buf[n + 2, :, cross]

    lower, upper = slice(0, wide), slice(wide, width)

    @pl.when(core == 0)
    def _():
        lay_out(lower, upper)

    @pl.when(core == 1)
    def _():
        lay_out(upper, lower)

    @pl.when(chip < chips // 2)
    def _():
        far_same[...] = kv_same[...]
        far_cross[...] = kv_cross[...]

    @pl.when(chip >= chips // 2)
    def _():
        far_same[...] = qd_same[...]
        far_cross[...] = qd_cross[...]


def prepare(lengths, queries, keys, values, gates, out_grad, chips):
    rows, width = queries.shape[1:]
    pair = jax.ShapeDtypeStruct((2, rows, width // 2), BF16)
    return pl.pallas_call(
        functools.partial(prep_kernel, chips=chips),
        out_shape=(pair,) * 6 + (jax.ShapeDtypeStruct((6, rows, width // 2), BF16),),
        in_specs=[SMEM] + [HBM] * 5,
        out_specs=(VMEM,) * 7,
        scratch_shapes=[pltpu.VMEM((5, rows, width), BF16), pltpu.SemaphoreType.DMA((5,))],
        compiler_params=pltpu.CompilerParams(vmem_limit_bytes=PREP_LIMIT),
        name="prep",
    )(lengths, queries, keys, values, gates, out_grad)


class Blocks:
    def __init__(self, cum, rab, span, depth, heads, bands, band_width, inv_root):
        self.cum, self.rab, self.span, self.depth, self.heads = cum, rab, span, depth, heads
        self.bands, self.band_width, self.inv_root = bands, band_width, inv_root
        self.rows = span // 2
        self.sub = min(self.rows, band_width)
        self.strips = self.rows // self.sub
        self.row_at = lax.broadcasted_iota(jnp.int32, (self.sub, span), 0)
        self.lane_at = lax.broadcasted_iota(jnp.int32, (self.sub, span), 1)
        self.lane_in = lax.rem(self.lane_at, self.sub)
        self.lane_strip = self.lane_at[:1, : self.rows] // self.sub

    def sum_steps(self, steps_ref, core):
        for head in range(self.heads):
            total = steps_ref[core * self.heads + head, 0]
            self.cum[head, 0] = total
            for level in range(1, self.bands):
                total = total + steps_ref[core * self.heads + head, level]
                self.cum[head, level] = total

    def level_of(self, gap, under):
        return jnp.clip(jnp.maximum(gap * self.sub - under, 0) // self.band_width, 0, self.bands - 1)

    def table(self, head, gap, sign, under):
        table = []
        for half in range(2):
            values = None
            for lane_no in range(self.strips):
                level = self.level_of(sign * (gap - half * self.strips - lane_no), under)
                value = jnp.full((1, self.rows), self.cum[head, level], F32)
                values = value if values is None else jnp.where(self.lane_strip == lane_no, value, values)
            table.append(values)
        return jnp.concatenate(table, axis=1)

    def run(self, left, right, gap, side, diagonal=False, acc=None):
        sign = 1 - 2 * side
        near = (self.row_at - self.lane_in) * sign >= 0
        for head in range(self.heads):
            cols = slice(head * self.depth, (head + 1) * self.depth)
            left_a, left_b = left(0, cols), left(1, cols)
            right_a, right_b = right(0, cols), right(1, cols)
            score = nt_dot(left_a, right_a)
            dweight = nt_dot(left_b, right_b)
            weights, dpres = [], []
            for strip in range(score.shape[0] // self.sub):
                part = slice(strip * self.sub, (strip + 1) * self.sub)
                bias = jnp.where(
                    near, self.table(head, gap + strip, sign, 0), self.table(head, gap + strip, sign, 1)
                )
                pre = score[part] * self.inv_root + bias
                bottom = 1.0 + jnp.exp2(jnp.maximum(pre, -87.0) * -1.4426950408889634)
                sig = pl.reciprocal(bottom, approx=True)
                sig = sig * (2.0 - bottom * sig)
                weight = pre * sig
                dpre = dweight[part] * (sig + weight * (1.0 - sig))
                if diagonal:
                    causal = (self.row_at + strip * self.sub - self.lane_at) * sign >= 0
                    weight = jnp.where(causal, weight, 0.0)
                    dpre = jnp.where(causal, dpre, 0.0)
                if acc is not None:
                    weights.append(weight.astype(BF16))
                    dpres.append(dpre.astype(BF16))
                whole = jnp.sum(dpre.reshape(self.sub // 8, 8, self.span), axis=0)
                inner = jnp.sum(jnp.where(near, dpre, 0.0).reshape(self.sub // 8, 8, self.span), axis=0)
                for half in range(2):
                    lanes = slice(half * self.rows, (half + 1) * self.rows)
                    for under, amount in ((0, inner[:, lanes]), (1, (whole - inner)[:, lanes])):
                        level = self.level_of(gap + strip - half * self.strips, under)
                        self.rab[head, jnp.where(side == 0, level, self.bands)] += amount
            if acc is not None:
                weight = jnp.concatenate(weights, axis=0)
                dpre = jnp.concatenate(dpres, axis=0)
                acc[side, 0, :, cols] += jnp.dot(weight, right_b, preferred_element_type=F32)
                acc[side, 1, :, cols] += jnp.dot(dpre, right_a, preferred_element_type=F32)

    def band_tile(self, out_ref, core, scale):
        lanes = lax.broadcasted_iota(jnp.int32, (self.bands, self.rows), 1) // self.sub
        level = lax.broadcasted_iota(jnp.int32, (self.bands, 128), 0)
        step_no = lax.broadcasted_iota(jnp.int32, (self.bands, 128), 1)
        out_ref[...] = jnp.zeros_like(out_ref)
        for head in range(self.heads):
            sums = jnp.sum(self.rab[head, : self.bands], axis=1)
            result = jnp.zeros((self.bands, 128), F32)
            for strip in range(self.strips):
                amount = jnp.sum(jnp.where(lanes == strip, sums, 0.0), axis=1, keepdims=True)
                result = result + jnp.where(level - strip >= step_no, amount, 0.0)
            row = jnp.sum(result, axis=0, keepdims=True) * scale
            row = jnp.broadcast_to(row, (out_ref.shape[0], 1, 128))
            for half in range(2):

                @pl.when(core == half)
                def _():
                    place = half * self.heads + head
                    out_ref[:, place : place + 1, :] = row


def position(rows):
    index = lax.axis_index("seq")
    chip, core = index // 2, lax.rem(index, 2)
    mine = pl.ds(pl.multiple_of(core * rows, rows), rows)
    others = pl.ds(pl.multiple_of((1 - core) * rows, rows), rows)
    return chip, core, mine, others


def first_kernel(
    steps_ref, kv_same, qd_same, near_ref, kv_ref, qd_ref, acc, rab, copied, cum, *, blocks_of
):
    rows = kv_same.shape[1]
    chip, core, mine, others = position(rows)
    copies = []
    for n in range(2):
        copies += [
            pltpu.make_async_copy(kv_same.at[n], kv_ref.at[n, mine], copied.at[0, n]),
            pltpu.make_async_copy(qd_same.at[n], qd_ref.at[n, mine], copied.at[1, n]),
            pltpu.make_async_copy(near_ref.at[n], kv_ref.at[n, others], copied.at[2, n]),
            pltpu.make_async_copy(near_ref.at[n + 2], qd_ref.at[n, others], copied.at[3, n]),
        ]
    for copy in copies:
        copy.start()
    acc[...] = jnp.zeros_like(acc)
    rab[...] = jnp.zeros_like(rab)
    blocks = blocks_of(cum, rab)
    blocks.sum_steps(steps_ref, core)
    for copy in copies:
        copy.wait()
    kv, qd = lambda n, cols: kv_ref[n, :, cols], lambda n, cols: qd_ref[n, :, cols]
    blocks.run(qd, kv, jnp.int32(0), 0, diagonal=True, acc=acc)
    blocks.run(kv, qd, jnp.int32(0), 1, diagonal=True, acc=acc)


def middle_kernel(*refs, ways, extra, blocks_of, scale):
    count = len(ways)
    steps_ref, kv_ref, qd_ref, acc_in, rab_in = refs[:5]
    pieces = refs[5 : 5 + 2 * count]
    acc, band_ref, stack, copied, rab, cum, plan = refs[5 + 2 * count :]
    rows = kv_ref.shape[1] // 2
    chip, core, mine, others = position(rows)
    chips = lax.axis_size("seq") // 2

    def arrivals(unit):
        return [
            pltpu.make_async_copy(pieces[2 * unit], stack.at[unit, :, mine], copied.at[0, unit]),
            pltpu.make_async_copy(pieces[2 * unit + 1], stack.at[unit, :, others], copied.at[1, unit]),
        ]

    for unit in range(count):
        for copy in arrivals(unit):
            copy.start()
    acc[...] = acc_in[...]
    rab[...] = rab_in[...]
    blocks = blocks_of(cum, rab)
    blocks.sum_steps(steps_ref, core)
    for unit, (way, hops) in enumerate(ways):
        below, above = chip >= hops, chip + hops < chips
        if way == "up":
            known, origin = below, chip - hops
        elif way == "down":
            known, origin = above, chip + hops
        else:
            known, origin = below | above, jnp.where(below, chip - hops, chip + hops)
        plan[unit] = jnp.where(known, origin, chip)
    for unit in range(count):
        for copy in arrivals(unit):
            copy.wait()
    per_chip = 2 * blocks.strips

    def step(unit, unused):
        origin = plan[unit]
        other = lambda n, cols: stack[unit, n, :, cols]
        gap = (chip - origin) * per_chip

        @pl.when(origin < chip)
        def _():
            blocks.run(lambda n, cols: qd_ref[n, :, cols], other, gap, 0, acc=acc)

        @pl.when(origin > chip)
        def _():
            blocks.run(lambda n, cols: kv_ref[n, :, cols], other, gap, 1, acc=acc)

        return unused

    lax.fori_loop(0, count, step, 0)

    up, down, far = extra
    half = chips // 2

    @pl.when((chip == half - 1) | (chip == half))
    def _():
        upper = chip - (half - 1)
        from_last = jnp.where(upper == 1, down, far)
        from_first = jnp.where(upper == 1, far, up)
        part = pl.ds(pl.multiple_of(upper * rows, rows), rows)
        blocks.run(
            lambda n, cols: stack[from_last, n, part, cols],
            lambda n, cols: stack[from_first, n, :, cols],
            (chips - 1) * per_chip + upper * blocks.strips,
            0,
        )

    blocks.band_tile(band_ref, core, scale)


def last_kernel(
    steps_ref, len_ref, kv_ref, qd_ref, acc_in, same_ref, cross_ref, near_ref, u_ref, og_ref,
    keep_ref, give_ref, stack, gate_buf, copied, acc, rab, cum,
    *, blocks_of, scale, inv_root,
):
    rows = kv_ref.shape[1] // 2
    wide = kv_ref.shape[2]
    chip, core, mine, others = position(rows)
    chips = lax.axis_size("seq") // 2
    copies = [
        pltpu.make_async_copy(same_ref, stack.at[:, mine], copied.at[0]),
        pltpu.make_async_copy(cross_ref, stack.at[:, others], copied.at[1]),
        pltpu.make_async_copy(near_ref.at[pl.ds(4, 2)], gate_buf, copied.at[2]),
    ]
    for copy in copies:
        copy.start()
    acc[...] = acc_in[...]
    blocks = blocks_of(cum, rab)
    blocks.sum_steps(steps_ref, core)
    for copy in copies:
        copy.wait()
    other = lambda n, cols: stack[n, :, cols]
    gap = (chips - 1) * 2 * blocks.strips

    @pl.when(chip == chips - 1)
    def _():
        blocks.run(lambda n, cols: qd_ref[n, :, cols], other, gap, 0, acc=acc)

    @pl.when(chip == 0)
    def _():
        blocks.run(lambda n, cols: kv_ref[n, :, cols], other, -gap, 1, acc=acc)

    def finish(out_ref, place, whose, gate, grad):
        start = (2 * chip + whose) * rows
        live = start + lax.broadcasted_iota(jnp.int32, (rows, 1), 0) < len_ref[0]
        attended = jnp.where(live, acc[0, 0, place] * scale, 0.0)
        out_ref[0] = (attended * gate.astype(F32)).astype(BF16)
        out_ref[1] = (acc[0, 1, place] * (scale * inv_root)).astype(BF16)
        out_ref[2] = (acc[1, 1, place] * (scale * inv_root)).astype(BF16)
        out_ref[3] = (acc[1, 0, place] * scale).astype(BF16)
        out_ref[4] = (attended * grad.astype(F32)).astype(BF16)

    finish(give_ref, others, 1 - core, gate_buf[0], gate_buf[1])
    for half in range(2):

        @pl.when(core == half)
        def _():
            cols = slice(half * wide, (half + 1) * wide)
            finish(keep_ref, mine, core, u_ref[0, :, cols], og_ref[0, :, cols])


def assemble_kernel(keep_ref, got_ref, *refs):
    outs, (buf, copied) = refs[:5], refs[5:]
    wide = keep_ref.shape[2]
    core = lax.rem(lax.axis_index("seq"), 2)
    for half in range(2):

        @pl.when(core == half)
        def _():
            buf[:, :, half * wide : (half + 1) * wide] = keep_ref[...]
            buf[:, :, (1 - half) * wide : (2 - half) * wide] = got_ref[...]

    copies = [pltpu.make_async_copy(buf.at[n], out.at[0], copied.at[n]) for n, out in enumerate(outs)]
    for copy in copies:
        copy.start()
    for copy in copies:
        copy.wait()


def params(units, span, wide, **more):
    return dict(
        compiler_params=pltpu.CompilerParams(vmem_limit_bytes=VMEM_LIMIT),
        cost_estimate=pl.CostEstimate(
            flops=int(units * 8 * span * span * wide * 10),
            bytes_accessed=int((units + 2) * 4 * span * wide),
            transcendentals=0,
        ),
        **more,
    )


def body(queries, keys, values, gates, lengths, rab_steps, out_grad, dp_size, seq_size):
    rows, width = queries.shape[1:]
    heads, bands = rab_steps.shape
    total_len = rows * seq_size
    chips, half = seq_size // 2, seq_size // 4
    span, wide, depth = 2 * rows, width // 2, width // heads
    inv_root, scale = depth**-0.5, total_len**-0.5
    blocks_of = functools.partial(
        Blocks, span=span, depth=depth, heads=heads // 2, bands=bands, band_width=total_len // bands, inv_root=inv_root
    )

    def send(value, hops, cross):
        pairs = [
            (2 * n + core, 2 * (n + far) + (1 - core if cross else core))
            for far, whence in hops
            for n in whence
            for core in range(2)
        ]
        return lax.ppermute(value, "seq", pairs)

    kv_same, kv_cross, qd_same, qd_cross, far_same, far_cross, near = prepare(
        lengths, queries, keys, values, gates, out_grad, chips
    )
    far_route = [(half, range(half)), (-half, range(half, chips))]
    across = [send(far_same, far_route, False), send(far_cross, far_route, True)]
    ways, pieces = [], []
    for hops in range(1, half):
        up, down = [(hops, range(chips - hops))], [(-hops, range(hops, chips))]
        ways += [("up", hops), ("down", hops)]
        pieces += [send(kv_same, up, False), send(kv_cross, up, True)]
        pieces += [send(qd_same, down, False), send(qd_cross, down, True)]
    extra = (len(ways) - 2, len(ways) - 1, len(ways))
    near = send(near, [(0, range(chips))], True)

    acc = jax.ShapeDtypeStruct((2, 2, span, wide), F32)
    rab = jax.ShapeDtypeStruct((heads // 2, bands + 1, 8, rows), F32)
    own = jax.ShapeDtypeStruct((2, span, wide), BF16)
    cum = pltpu.SMEM((heads // 2, bands), F32)
    own_kv, own_qd, acc_now, rab_now = pl.pallas_call(
        functools.partial(first_kernel, blocks_of=blocks_of),
        out_shape=(own, own, acc, rab),
        in_specs=[SMEM, ANY, ANY, ANY],
        out_specs=(VMEM,) * 4,
        scratch_shapes=[pltpu.SemaphoreType.DMA((4, 2)), cum],
        **params(2, span, wide, name="attend_own"),
    )(rab_steps, kv_same, qd_same, near)

    acc_now, across = lax.optimization_barrier((acc_now, across))
    for hops in range(half, chips - 1):
        ways.append(("either", hops))
        pieces += across
        onward = [(1, range(hops, chips - 1)), (-1, range(1, chips - hops))]
        across = [send(value, onward, False) for value in across]
    count = dp_size * seq_size
    together = count <= 64
    acc_now, band = pl.pallas_call(
        functools.partial(middle_kernel, ways=tuple(ways), extra=extra, blocks_of=blocks_of, scale=scale),
        out_shape=(acc, jax.ShapeDtypeStruct((count if together else seq_size, 8, 128), F32)),
        in_specs=[SMEM] + [VMEM] * 4 + [ANY] * len(pieces),
        out_specs=(VMEM,) * 2,
        scratch_shapes=[
            pltpu.VMEM((len(ways), 2, span, wide), BF16),
            pltpu.SemaphoreType.DMA((2, len(ways))),
            pltpu.VMEM(rab.shape, F32),
            cum,
            pltpu.SMEM((len(ways),), jnp.int32),
        ],
        **params(len(ways), span, wide, name="attend_middle"),
    )(rab_steps, own_kv, own_qd, acc_now, rab_now, *pieces)
    band = lax.all_to_all(band, ("dp", "seq") if together else "seq", 0, 0)

    band, across = lax.optimization_barrier((band, across))
    half_out = jax.ShapeDtypeStruct((5, rows, wide), BF16)
    keep, give = pl.pallas_call(
        functools.partial(last_kernel, blocks_of=blocks_of, scale=scale, inv_root=inv_root),
        out_shape=(half_out, half_out),
        in_specs=[SMEM, SMEM] + [VMEM] * 3 + [ANY] * 3 + [VMEM] * 2,
        out_specs=(VMEM,) * 2,
        scratch_shapes=[
            pltpu.VMEM((2, span, wide), BF16),
            pltpu.VMEM((2, rows, wide), BF16),
            pltpu.SemaphoreType.DMA((3,)),
            pltpu.VMEM(acc.shape, F32),
            pltpu.VMEM(rab.shape, F32),
            cum,
        ],
        **params(1, span, wide, name="attend_last"),
    )(rab_steps, lengths, own_kv, own_qd, acc_now, *across, near, gates, out_grad)
    got = send(give, [(0, range(chips))], True)
    out = jax.ShapeDtypeStruct(queries.shape, BF16)
    outs = pl.pallas_call(
        assemble_kernel,
        out_shape=(out,) * 5,
        in_specs=[VMEM, VMEM],
        out_specs=(HBM,) * 5,
        scratch_shapes=[pltpu.VMEM((5, rows, width), BF16), pltpu.SemaphoreType.DMA((5,))],
        compiler_params=pltpu.CompilerParams(vmem_limit_bytes=VMEM_LIMIT),
        name="assemble",
    )(keep, got)
    band = jnp.sum(band, axis=0)
    if not together:
        band = lax.psum(band, "dp")
    return (*outs, band[:heads, :bands] / total_len)


def solution(mesh):
    rows = P("dp", "seq", None)
    return jax.shard_map(
        functools.partial(body, dp_size=mesh.shape["dp"], seq_size=mesh.shape["seq"]),
        mesh=mesh,
        in_specs=(rows, rows, rows, rows, P("dp"), P(), rows),
        out_specs=(rows, rows, rows, rows, rows, P()),
        check_vma=False,
    )
```

time: 191 us -> 54.5 us (0.29)
  blocking collectives: 51.2 us -> 0 us
  local copies, waits for them, and re-layouts: 34.4 us -> 1.82 us
  waiting for transfers between devices: 48.1 us -> 16.4 us
  starting transfers between devices: 0.16 us -> 22.1 us
  matrix products: 18.6 us -> 0 us
  other arithmetic: 14.3 us -> 0.62 us
  between operations: 14.5 us -> 1.46 us
  Pallas kernels: 0 us -> 11.8 us
  loops' own time: 9.25 us -> 0 us
    psum x1 -> x0, blocking collectives: 51.2 us -> none  [body(): rab_grad = lax.psum(rab_acc, ('dp', 'seq')) / total_len]
    all_gather x4 -> x0, waiting for transfers between devices: 48 us -> none  [the longest x1 24.8 us: body(): lax.all_gather(own_value, 'seq', axis=0, tiled=True)]
    dot_general x10 -> x0, matrix products: 18.6 us -> none  [the longest x3 8.81 us: pair_terms(): jnp.einsum('ihd,jhd->hij', split_heads(query_rows, head_count), split_hea...]
    ppermute x0 -> x10, waiting for transfers between devices: none -> 16.4 us  [send(): return lax.ppermute(value, 'seq', pairs)]
    ppermute x0 -> x10, starting transfers between devices: none -> 15.4 us  [send(): return lax.ppermute(value, 'seq', pairs)]
    pallas_call x0 -> x5, Pallas kernels: none -> 11.8 us  [the longest x1 3.73 us: body(): pl.pallas_call(functools.partial(middle_kernel, ways=tuple(ways), extra=e...]
    dynamic_slice x13 -> x0, local copies, waits for them, and re-layouts: 9.49 us -> none  [the longest x3 4.02 us: inner(): first_part = lax.dynamic_slice_in_dim(pieces[0], begin, sub_rows, 0)]
    another operation x6 -> x0, loops' own time: 9.25 us -> none  [the longest x2 5.4 us: in_blocks(): lax.scan(inner, carry, jnp.arange(total_rows // sub_rows, dtype=jnp.int32))]
  transfers between devices with their start and end apart: 4 -> 11, of which waited for: 3 -> 5; matrix products, arithmetic and copies ran while one was open for 10% -> 1% of each run, Pallas kernels for 0% -> 5%
where the time goes in v1:
time: 54.5 us; the launch traced here: 54.1 us
  starting transfers between devices  22.1 us (41%)
  waiting for transfers between devices  16.4 us (30%)
  Pallas kernels  11.8 us (22%)
  local copies, waits for them, and re-layouts  1.82 us (3%)
  between operations  1.46 us (3%)
  other arithmetic  0.62 us (1%)
    ppermute x10, waiting for transfers between devices, send(): return lax.ppermute(value, 'seq', pairs)  16.4 us
    ppermute x10, starting transfers between devices, send(): return lax.ppermute(value, 'seq', pairs)  15.4 us
    all_to_all x1, starting transfers between devices, body(): band = lax.all_to_all(band, ('dp', 'seq') if together else 'seq', 0, 0)  6.66 us
    pallas_call x1, Pallas kernels, body(): pl.pallas_call(functools.partial(middle_kernel, ways=tuple(ways), extra=e...  3.73 us
    pallas_call x1, Pallas kernels, body(): pl.pallas_call(functools.partial(first_kernel, blocks_of=blocks_of), out_...  2.84 us
    pallas_call x1, Pallas kernels, prepare(): pl.pallas_call(functools.partial(prep_kernel, chips=chips), out_shape=(pa...  2.33 us
    pallas_call x1, Pallas kernels, body(): pl.pallas_call(functools.partial(last_kernel, blocks_of=blocks_of, scale=...  1.93 us
    unnamed x10, local copies, waits for them, and re-layouts  1.82 us
  transfers between devices with their start and end apart: 11, of which 5 were waited for; matrix products, arithmetic and copies ran while one was open for 1% of the time, Pallas kernels for 5%

profile of v1, /device:TPU:0, one launch (start us, length us, event | category | flops | bytes accessed | tf_op | source)
XLA Modules:
  0.0 54.1 jit_solution(16234250505533799858)
XLA Ops:
  1.3 2.3 %prep.1 = (bf16[2,128,256]{2,1,0:T(8,128)(2,1)}, bf16[2,128,256]{2,1,0:T(8,128)(2,1)}, bf16[2,128,256]{2,1,0:T(8,128)(2,1)}, bf16[2,128,256]{2,1,0:T(8,128)(2,1)...) custom-call(s32[1]{0:T(128)S(6)} %copy.13.len_ref, ...), custom_call_target="tpu_custom_call" | custom-call | tf_op jit(solution)/shard_map/prep/pallas_call | solution.py:81
  3.6 0.5 collective-permute-start
  4.1 3.7 %collective-permute-start.1 = (bf16[2,128,256]{2,1,0:T(8,128)(2,1)}, bf16[2,128,256]{2,1,0:T(8,128)(2,1)S(1)}, u32[]{:S(2)}, u32[]{:S(2)}) collective-permute-start(bf16[2,128,256]{2,1,0:T(8,128)(2,1)} %get-tuple-element.38), channel_id=1, source_target_pairs={{0,4},{1,5},{2,6},{3,7},{4,0},{5,1},{6,2},{7,3},{8,12},{9,13},{10,... | collective-permute-start | bytes 393224 | tf_op jit(solution)/shard_map/ppermute | solution.py:393
  7.8 0.1 collective-permute-start.2
  7.9 3.5 %collective-permute-start.4 = (bf16[2,128,256]{2,1,0:T(8,128)(2,1)}, bf16[2,128,256]{2,1,0:T(8,128)(2,1)S(1)}, u32[]{:S(2)}, u32[]{:S(2)}) collective-permute-start(bf16[2,128,256]{2,1,0:T(8,128)(2,1)} %get-tuple-element.42), channel_id=1, source_target_pairs={{0,3},{1,2},{2,5},{3,4},{4,7},{5,6},{8,11},{9,10},{10,13},{11,12},... | collective-permute-start | bytes 393224 | tf_op jit(solution)/shard_map/ppermute | solution.py:393
  11.3 0.0 copy-start.4
  11.4 1.3 %collective-permute-start.6 = (bf16[2,128,256]{2,1,0:T(8,128)(2,1)}, bf16[2,128,256]{2,1,0:T(8,128)(2,1)S(1)}, u32[]{:S(2)}, u32[]{:S(2)}) collective-permute-start(bf16[2,128,256]{2,1,0:T(8,128)(2,1)} %get-tuple-element.43), channel_id=1, source_target_pairs={{2,1},{3,0},{4,3},{5,2},{6,5},{7,4},{10,9},{11,8},{12,11},{13,10},... | collective-permute-start | bytes 393224 | tf_op jit(solution)/shard_map/ppermute | solution.py:393
  12.7 5.4 %collective-permute-done.1.refs_9_ = bf16[2,128,256]{2,1,0:T(8,128)(2,1)S(1)} collective-permute-done((bf16[2,128,256]{2,1,0:T(8,128)(2,1)}, bf16[2,128,256]{2,1,0:T(8,128)(2,1)S(1)}, u32[]{:S(2)}, u32[]{:S(2)}) %collective-permute-start.1) | collective-permute-done | bytes 131104 | tf_op jit(solution)/shard_map/ppermute | solution.py:393
  18.1 2.5 %collective-permute-start.3 = (bf16[2,128,256]{2,1,0:T(8,128)(2,1)}, bf16[2,128,256]{2,1,0:T(8,128)(2,1)S(1)}, u32[]{:S(2)}, u32[]{:S(2)}) collective-permute-start(bf16[2,128,256]{2,1,0:T(8,128)(2,1)} %get-tuple-element.32.kv_same), channel_id=1, source_target_pairs={{0,2},{1,3},{2,4},{3,5},{4,6},{5,7},{8,10},{9,11},{10,12},{11,13},... | collective-permute-start | bytes 393224 | tf_op jit(solution)/shard_map/ppermute | solution.py:393
  20.6 0.0 collective-permute-done.near_ref
  20.6 1.3 %collective-permute-start.5 = (bf16[2,128,256]{2,1,0:T(8,128)(2,1)}, bf16[2,128,256]{2,1,0:T(8,128)(2,1)S(1)}, u32[]{:S(2)}, u32[]{:S(2)}) collective-permute-start(bf16[2,128,256]{2,1,0:T(8,128)(2,1)} %get-tuple-element.33.qd_same), channel_id=1, source_target_pairs={{2,0},{3,1},{4,2},{5,3},{6,4},{7,5},{10,8},{11,9},{12,10},{13,11},... | collective-permute-start | bytes 393224 | tf_op jit(solution)/shard_map/ppermute | solution.py:393
  21.9 0.0 copy-start.2
  21.9 0.9 %copy-done.2 = bf16[2,128,256]{2,1,0:T(8,128)(2,1)S(1)} copy-done((bf16[2,128,256]{2,1,0:T(8,128)(2,1)S(1)}, bf16[2,128,256]{2,1,0:T(8,128)(2,1)}, u32[]{:S(2)}) %copy-start.2) | copy-done | bytes 131096
  22.8 0.9 %copy-done.3 = bf16[2,128,256]{2,1,0:T(8,128)(2,1)S(1)} copy-done((bf16[2,128,256]{2,1,0:T(8,128)(2,1)S(1)}, bf16[2,128,256]{2,1,0:T(8,128)(2,1)}, u32[]{:S(2)}) %copy-start.3) | copy-done | bytes 131096
  23.7 2.8 %attend_own.1 = (bf16[2,256,256]{2,1,0:T(8,128)(2,1)S(1)}, bf16[2,256,256]{2,1,0:T(8,128)(2,1)S(1)}, f32[2,2,256,256]{3,2,1,0:T(8,128)S(1)}, f32[2,17,8,128]{3,2,1,0:T(8,128)S(1)}) custom-call(f32[4,16]{1,0:T(4,128)S(1)} %copy-done.4, bf16[2,128,256]{2,1,0:T(8,128)(2,1)S(1)} %copy-done.3, bf16[2,128,256]{2,1,0:T(8,128)(2,1)S(1)} %copy-done.2, ...), custom_call_target="tpu_custom_call" | custom-call | flops 2684354560 | bytes 1048576 | tf_op jit(solution)/shard_map/attend_own/pallas_call | solution.py:413
  26.5 0.0 collective-permute-done.2.refs_10_
  26.6 0.0 collective-permute-done.4.refs_6_
  26.6 1.2 %collective-permute-done.5.refs_7_ = bf16[2,128,256]{2,1,0:T(8,128)(2,1)S(1)} collective-permute-done((bf16[2,128,256]{2,1,0:T(8,128)(2,1)}, bf16[2,128,256]{2,1,0:T(8,128)(2,1)S(1)}, u32[]{:S(2)}, u32[]{:S(2)}) %collective-permute-start.5) | collective-permute-done | bytes 131104 | tf_op jit(solution)/shard_map/ppermute | solution.py:393
  27.8 3.7 %attend_middle.1 = (f32[2,2,256,256]{3,2,1,0:T(8,128)S(1)}, f32[32,8,128]{2,1,0:T(8,128)}) custom-call(f32[4,16]{1,0:T(4,128)S(1)} %copy-done.4, bf16[2,256,256]{2,1,0:T(8,128)(2,1)S(1)} %get-tuple-element.35.refs_1_.kv_ref, bf16[2,256,256]{2,1,0:T(8,128)(2,1)S(1)} %get-tuple-element.36.refs_2_.qd_ref, f32[2,2,256,256]{3,2,1,0:T(8,128)S(1)} %get-tuple-element.40.refs_3_, ...), custom_call_target="tpu_custom_call" | custom-call | flops 4026531840 | bytes 1310720 | tf_op jit(solution)/shard_map/attend_middle/pallas_call | solution.py:430
  31.6 0.0 copy-start
  31.6 0.0 copy-start.1
  31.6 6.7 %all-to-all-start = ((f32[32,8,128]{2,1,0:T(8,128)}), f32[32,8,128]{2,1,0:T(8,128)S(1)}, u32[]{:S(2)}, u32[]{:S(2)}) async-start(f32[32,8,128]{2,1,0:T(8,128)} %get-tuple-element.47), calls=%async_computation | async-start | bytes 262144 | tf_op jit(solution)/shard_map/all_to_all | solution.py:444
  38.3 1.3 %collective-permute-start.7 = (bf16[2,128,256]{2,1,0:T(8,128)(2,1)S(1)}, bf16[2,128,256]{2,1,0:T(8,128)(2,1)S(1)}, u32[]{:S(2)}, u32[]{:S(2)}) collective-permute-start(bf16[2,128,256]{2,1,0:T(8,128)(2,1)S(1)} %collective-permute-done.1.refs_9_), channel_id=1, source_target_pairs={{4,6},{5,7},{2,0},{3,1},{12,14},{13,15},{10,8},{11,9},{20,22},{21,... | collective-permute-start | bytes 393224 | tf_op jit(solution)/shard_map/ppermute | solution.py:393
  39.6 1.3 %collective-permute-start.8 = (bf16[2,128,256]{2,1,0:T(8,128)(2,1)S(1)}, bf16[2,128,256]{2,1,0:T(8,128)(2,1)S(1)}, u32[]{:S(2)}, u32[]{:S(2)}) collective-permute-start(bf16[2,128,256]{2,1,0:T(8,128)(2,1)S(1)} %collective-permute-done.2.refs_10_), channel_id=1, source_target_pairs={{4,6},{5,7},{2,0},{3,1},{12,14},{13,15},{10,8},{11,9},{20,22},{21,... | collective-permute-start | bytes 393224 | tf_op jit(solution)/shard_map/ppermute | solution.py:393
  40.9 6.2 %collective-permute-done.7.same_ref = bf16[2,128,256]{2,1,0:T(8,128)(2,1)S(1)} collective-permute-done((bf16[2,128,256]{2,1,0:T(8,128)(2,1)S(1)}, bf16[2,128,256]{2,1,0:T(8,128)(2,1)S(1)}, u32[]{:S(2)}, u32[]{:S(2)}) %collective-permute-start.7) | collective-permute-done | bytes 131104 | tf_op jit(solution)/shard_map/ppermute | solution.py:393
  47.1 2.5 %collective-permute-done.8.cross_ref = bf16[2,128,256]{2,1,0:T(8,128)(2,1)S(1)} collective-permute-done((bf16[2,128,256]{2,1,0:T(8,128)(2,1)S(1)}, bf16[2,128,256]{2,1,0:T(8,128)(2,1)S(1)}, u32[]{:S(2)}, u32[]{:S(2)}) %collective-permute-start.8) | collective-permute-done | bytes 131104 | tf_op jit(solution)/shard_map/ppermute | solution.py:393
  49.6 0.0 all-to-all-done
  49.6 1.9 %attend_last.1 = (bf16[5,128,256]{2,1,0:T(8,128)(2,1)S(1)}, bf16[5,128,256]{2,1,0:T(8,128)(2,1)S(1)}) custom-call(f32[4,16]{1,0:T(4,128)S(1)} %copy-done.4, s32[1]{0:T(128)S(6)} %copy.13.len_ref, bf16[2,256,256]{2,1,0:T(8,128)(2,1)S(1)} %get-tuple-element.35.refs_1_.kv_ref, bf16[2,256,256]{2,1,0:T(8,128)(2,1)S(1)} %get-tuple-element.36.refs_2_.qd_ref, ...), custom_call_target="tpu_custom_call" | custom-call | flops 1342177280 | bytes 786432 | tf_op jit(solution)/shard_map/attend_last/pallas_call | solution.py:448
  51.5 0.1 collective-permute-start.9
  51.6 0.6 %slice_multiply_fusion = f32[4,16]{1,0:T(4,128)} fusion(f32[8,128]{1,0:T(8,128)S(1)} %reduce_sum.9), kind=kLoop, calls=%fused_computation | loop fusion | flops 64 | bytes 512 | tf_op jit(solution)/shard_map/div | solution.py:477
  52.2 1.0 %collective-permute-done.9.got_ref = bf16[5,128,256]{2,1,0:T(8,128)(2,1)S(1)} collective-permute-done((bf16[5,128,256]{2,1,0:T(8,128)(2,1)S(1)}, bf16[5,128,256]{2,1,0:T(8,128)(2,1)S(1)}, u32[]{:S(2)}, u32[]{:S(2)}) %collective-permute-start.9) | collective-permute-done | bytes 327712 | tf_op jit(solution)/shard_map/ppermute | solution.py:393
  53.2 0.9 %assemble.1 = (bf16[1,128,512]{2,1,0:T(8,128)(2,1)}, bf16[1,128,512]{2,1,0:T(8,128)(2,1)}, bf16[1,128,512]{2,1,0:T(8,128)(2,1)}, bf16[1,128,512]{2,1,0:T(8,128)(2,1)}, bf16[1,128,512]{2,1,0:T(8,128)(2,1)}) custom-call(bf16[5,128,256]{2,1,0:T(8,128)(2,1)S(1)} %get-tuple-element.50.keep_ref, bf16[5,128,256]{2,1,0:T(8,128)(2,1)S(1)} %collective-permute-done.9.got_ref), custom_call_target="tpu_custom_call" | custom-call | tf_op jit(solution)/shard_map/assemble/pallas_call | solution.py:465
  (7 shorter events, 0.0 us)
Async XLA Ops:
  3.6 16.9 %collective-permute-start = (bf16[6,128,256]{2,1,0:T(8,128)(2,1)}, bf16[6,128,256]{2,1,0:T(8,128)(2,1)S(1)}, u32[]{:S(2)}, u32[]{:S(2)}) collective-permute-start(bf16[6,128,256]{2,1,0:T(8,128)(2,1)} %get-tuple-element.34), channel_id=1, source_target_pairs={{0,1},{1,0},{2,3},{3,2},{4,5},{5,4},{6,7},{7,6},{8,9},{9,8},{10,11... | collective-permute-start | bytes 1179656 | tf_op jit(solution)/shard_map/ppermute | solution.py:393
  4.1 13.9 %collective-permute-start.1 = (bf16[2,128,256]{2,1,0:T(8,128)(2,1)}, bf16[2,128,256]{2,1,0:T(8,128)(2,1)S(1)}, u32[]{:S(2)}, u32[]{:S(2)}) collective-permute-start(bf16[2,128,256]{2,1,0:T(8,128)(2,1)} %get-tuple-element.38), channel_id=1, source_target_pairs={{0,4},{1,5},{2,6},{3,7},{4,0},{5,1},{6,2},{7,3},{8,12},{9,13},{10,... | collective-permute-start | bytes 393224 | tf_op jit(solution)/shard_map/ppermute | solution.py:393
  7.8 18.7 %collective-permute-start.2 = (bf16[2,128,256]{2,1,0:T(8,128)(2,1)}, bf16[2,128,256]{2,1,0:T(8,128)(2,1)S(1)}, u32[]{:S(2)}, u32[]{:S(2)}) collective-permute-start(bf16[2,128,256]{2,1,0:T(8,128)(2,1)} %get-tuple-element.39), channel_id=1, source_target_pairs={{0,5},{1,4},{2,7},{3,6},{4,1},{5,0},{6,3},{7,2},{8,13},{9,12},{10,... | collective-permute-start | bytes 393224 | tf_op jit(solution)/shard_map/ppermute | solution.py:393
  7.9 18.7 %collective-permute-start.4 = (bf16[2,128,256]{2,1,0:T(8,128)(2,1)}, bf16[2,128,256]{2,1,0:T(8,128)(2,1)S(1)}, u32[]{:S(2)}, u32[]{:S(2)}) collective-permute-start(bf16[2,128,256]{2,1,0:T(8,128)(2,1)} %get-tuple-element.42), channel_id=1, source_target_pairs={{0,3},{1,2},{2,5},{3,4},{4,7},{5,6},{8,11},{9,10},{10,13},{11,12},... | collective-permute-start | bytes 393224 | tf_op jit(solution)/shard_map/ppermute | solution.py:393
  11.3 10.5 %copy-start.4 = (f32[4,16]{1,0:T(4,128)S(1)}, f32[4,16]{1,0:T(4,128)}, u32[]{:S(2)}) copy-start(f32[4,16]{1,0:T(4,128)} %steps_ref.3) | copy-start | bytes 772
  11.4 15.2 %collective-permute-start.6 = (bf16[2,128,256]{2,1,0:T(8,128)(2,1)}, bf16[2,128,256]{2,1,0:T(8,128)(2,1)S(1)}, u32[]{:S(2)}, u32[]{:S(2)}) collective-permute-start(bf16[2,128,256]{2,1,0:T(8,128)(2,1)} %get-tuple-element.43), channel_id=1, source_target_pairs={{2,1},{3,0},{4,3},{5,2},{6,5},{7,4},{10,9},{11,8},{12,11},{13,10},... | collective-permute-start | bytes 393224 | tf_op jit(solution)/shard_map/ppermute | solution.py:393
  18.1 8.5 %collective-permute-start.3 = (bf16[2,128,256]{2,1,0:T(8,128)(2,1)}, bf16[2,128,256]{2,1,0:T(8,128)(2,1)S(1)}, u32[]{:S(2)}, u32[]{:S(2)}) collective-permute-start(bf16[2,128,256]{2,1,0:T(8,128)(2,1)} %get-tuple-element.32.kv_same), channel_id=1, source_target_pairs={{0,2},{1,3},{2,4},{3,5},{4,6},{5,7},{8,10},{9,11},{10,12},{11,13},... | collective-permute-start | bytes 393224 | tf_op jit(solution)/shard_map/ppermute | solution.py:393
  20.6 7.2 %collective-permute-start.5 = (bf16[2,128,256]{2,1,0:T(8,128)(2,1)}, bf16[2,128,256]{2,1,0:T(8,128)(2,1)S(1)}, u32[]{:S(2)}, u32[]{:S(2)}) collective-permute-start(bf16[2,128,256]{2,1,0:T(8,128)(2,1)} %get-tuple-element.33.qd_same), channel_id=1, source_target_pairs={{2,0},{3,1},{4,2},{5,3},{6,4},{7,5},{10,8},{11,9},{12,10},{13,11},... | collective-permute-start | bytes 393224 | tf_op jit(solution)/shard_map/ppermute | solution.py:393
  21.9 0.9 %copy-start.2 = (bf16[2,128,256]{2,1,0:T(8,128)(2,1)S(1)}, bf16[2,128,256]{2,1,0:T(8,128)(2,1)}, u32[]{:S(2)}) copy-start(bf16[2,128,256]{2,1,0:T(8,128)(2,1)} %get-tuple-element.33.qd_same) | copy-start | bytes 393220
  22.8 0.9 %copy-start.3 = (bf16[2,128,256]{2,1,0:T(8,128)(2,1)S(1)}, bf16[2,128,256]{2,1,0:T(8,128)(2,1)}, u32[]{:S(2)}) copy-start(bf16[2,128,256]{2,1,0:T(8,128)(2,1)} %get-tuple-element.32.kv_same) | copy-start | bytes 393220
  31.6 18.0 %copy-start = (bf16[1,128,512]{2,1,0:T(8,128)(2,1)S(1)}, bf16[1,128,512]{2,1,0:T(8,128)(2,1)}, u32[]{:S(2)}) copy-start(bf16[1,128,512]{2,1,0:T(8,128)(2,1)} %u_ref.3) | copy-start | bytes 393220
  31.6 18.0 %copy-start.1 = (bf16[1,128,512]{2,1,0:T(8,128)(2,1)S(1)}, bf16[1,128,512]{2,1,0:T(8,128)(2,1)}, u32[]{:S(2)}) copy-start(bf16[1,128,512]{2,1,0:T(8,128)(2,1)} %og_ref.3) | copy-start | bytes 393220
  31.6 18.0 %all-to-all-start = ((f32[32,8,128]{2,1,0:T(8,128)}), f32[32,8,128]{2,1,0:T(8,128)S(1)}, u32[]{:S(2)}, u32[]{:S(2)}) async-start(f32[32,8,128]{2,1,0:T(8,128)} %get-tuple-element.47), calls=%async_computation | async-start | bytes 262144 | tf_op jit(solution)/shard_map/all_to_all | solution.py:444
  38.3 8.8 %collective-permute-start.7 = (bf16[2,128,256]{2,1,0:T(8,128)(2,1)S(1)}, bf16[2,128,256]{2,1,0:T(8,128)(2,1)S(1)}, u32[]{:S(2)}, u32[]{:S(2)}) collective-permute-start(bf16[2,128,256]{2,1,0:T(8,128)(2,1)S(1)} %collective-permute-done.1.refs_9_), channel_id=1, source_target_pairs={{4,6},{5,7},{2,0},{3,1},{12,14},{13,15},{10,8},{11,9},{20,22},{21,... | collective-permute-start | bytes 393224 | tf_op jit(solution)/shard_map/ppermute | solution.py:393
  39.6 10.0 %collective-permute-start.8 = (bf16[2,128,256]{2,1,0:T(8,128)(2,1)S(1)}, bf16[2,128,256]{2,1,0:T(8,128)(2,1)S(1)}, u32[]{:S(2)}, u32[]{:S(2)}) collective-permute-start(bf16[2,128,256]{2,1,0:T(8,128)(2,1)S(1)} %collective-permute-done.2.refs_10_), channel_id=1, source_target_pairs={{4,6},{5,7},{2,0},{3,1},{12,14},{13,15},{10,8},{11,9},{20,22},{21,... | collective-permute-start | bytes 393224 | tf_op jit(solution)/shard_map/ppermute | solution.py:393
  51.5 1.7 %collective-permute-start.9 = (bf16[5,128,256]{2,1,0:T(8,128)(2,1)S(1)}, bf16[5,128,256]{2,1,0:T(8,128)(2,1)S(1)}, u32[]{:S(2)}, u32[]{:S(2)}) collective-permute-start(bf16[5,128,256]{2,1,0:T(8,128)(2,1)S(1)} %get-tuple-element.51), channel_id=1, source_target_pairs={{0,1},{1,0},{2,3},{3,2},{4,5},{5,4},{6,7},{7,6},{8,9},{9,8},{10,11... | collective-permute-start | bytes 983048 | tf_op jit(solution)/shard_map/ppermute | solution.py:393

commit v2 on v1

v2 whole, which is shorter than its diff:
```python
import functools

import jax
import jax.numpy as jnp
from jax import lax
from jax.experimental import pallas as pl
from jax.experimental.pallas import tpu as pltpu
from jax.sharding import PartitionSpec as P

F32 = jnp.float32
BF16 = jnp.bfloat16
VMEM = pl.BlockSpec(memory_space=pltpu.VMEM)
SMEM = pl.BlockSpec(memory_space=pltpu.SMEM)
HBM = pl.BlockSpec(memory_space=pltpu.HBM)
ANY = pl.BlockSpec(memory_space=pl.ANY)
VMEM_LIMIT = 40 * 1024 * 1024
PREP_LIMIT = 60 * 1024 * 1024


def nt_dot(left, right):
    return lax.dot_general(left, right, (((1,), (1,)), ((), ())), preferred_element_type=F32)


class Round:
    def __init__(self, chips, payload, route, earlier=()):
        self.payload, self.route = payload, route
        self.origin = list(range(chips))
        for source, target in route.items():
            self.origin[target] = source if isinstance(payload, str) else earlier[payload].origin[source]


def plan_rounds(chips):
    half = chips // 2
    early, late = [], []

    def add(rounds, payload, route):
        rounds.append(Round(chips, payload, route, early))
        return len(rounds) - 1

    if chips == 4:
        across = add(early, "even", {0: 2, 3: 1, 1: 0, 2: 3})
        inner = add(early, "low", {1: 2, 2: 1})
        outer = add(early, "low", {0: 1, 3: 2})
        add(late, across, {2: 3, 1: 0})
        add(late, inner, {2: 3, 1: 0})
        return early, late, {across: (1,)}, {1: (across, outer, 0), 2: (outer, across, 1)}
    far = add(early, "low", {n: n + half if n < half else n - half for n in range(chips)})
    for hops in range(1, half):
        up = add(early, "kv", {n: n + hops for n in range(chips - hops)})
        down = add(early, "qd", {n: n - hops for n in range(hops, chips)})
    held = far
    for hops in range(half, chips - 1):
        route = {n: n + 1 for n in range(hops, chips - 1)} | {n: n - 1 for n in range(1, chips - hops)}
        held = add(early if hops < chips - 2 else late, held, route)
    return early, late, {}, {half - 1: (far, up, 0), half: (down, far, 1)}


def of_chip(table, chip):
    result = jnp.int32(table[0])
    for n in range(1, len(table)):
        result = jnp.where(chip == n, jnp.int32(table[n]), result)
    return result


def prep_kernel(len_ref, k_ref, v_ref, q_ref, u_ref, og_ref, same_ref, cross_ref, buf, copied):
    copies = [
        pltpu.make_async_copy(source.at[0], buf.at[n], copied.at[n])
        for n, source in enumerate((k_ref, v_ref, q_ref, u_ref, og_ref))
    ]
    for copy in copies:
        copy.start()
    rows, width = buf.shape[1:]
    wide = width // 2
    index = lax.axis_index("seq")
    live = index * rows + lax.broadcasted_iota(jnp.int32, (rows, 1), 0) < len_ref[0]
    for copy in copies:
        copy.wait()
    for half in range(2):
        cols = slice(half * wide, (half + 1) * wide)
        grad = buf[3, :, cols].astype(F32) * buf[4, :, cols].astype(F32)
        grad = jnp.where(live, grad, 0.0).astype(BF16)

        def lay_out(out_ref):
            for n in range(3):
                out_ref[n] = buf[n, :, cols]
            out_ref[3] = grad
            out_ref[4] = buf[3, :, cols]
            out_ref[5] = buf[4, :, cols]

        @pl.when(lax.rem(index, 2) == half)
        def _():
            lay_out(same_ref)

        @pl.when(lax.rem(index, 2) != half)
        def _():
            lay_out(cross_ref)


def build_kernel(same_ref, near_ref, kv_ref, qd_ref, gate_ref, low_ref, even_ref, *, chips):
    chip, _, mine, others = position(same_ref.shape[1])
    for place, source in ((mine, same_ref), (others, near_ref)):
        for n, out_ref in enumerate((kv_ref, qd_ref, gate_ref)):
            out_ref[0, place] = source[2 * n]
            out_ref[1, place] = source[2 * n + 1]

    for out_ref, keys_go in ((low_ref, chip < chips // 2), (even_ref, lax.rem(chip, 2) == 0)):

        @pl.when(keys_go)
        def _():
            out_ref[...] = kv_ref[...]

        @pl.when(jnp.logical_not(keys_go))
        def _():
            out_ref[...] = qd_ref[...]


class Blocks:
    def __init__(self, cum, rab, span, depth, heads, bands, band_width, inv_root):
        self.cum, self.rab, self.span, self.depth, self.heads = cum, rab, span, depth, heads
        self.bands, self.band_width, self.inv_root = bands, band_width, inv_root
        self.rows = span // 2
        self.sub = min(self.rows, band_width)
        self.strips = self.rows // self.sub
        self.row_at = lax.broadcasted_iota(jnp.int32, (self.sub, span), 0)
        self.lane_at = lax.broadcasted_iota(jnp.int32, (self.sub, span), 1)
        self.lane_in = lax.rem(self.lane_at, self.sub)
        self.lane_strip = self.lane_at[:1, : self.rows] // self.sub

    def sum_steps(self, steps_ref, core):
        for head in range(self.heads):
            total = steps_ref[core * self.heads + head, 0]
            self.cum[head, 0] = total
            for level in range(1, self.bands):
                total = total + steps_ref[core * self.heads + head, level]
                self.cum[head, level] = total

    def level_of(self, gap, under):
        return jnp.clip(jnp.maximum(gap * self.sub - under, 0) // self.band_width, 0, self.bands - 1)

    def table(self, head, gap, sign, under):
        table = []
        for half in range(2):
            values = None
            for lane_no in range(self.strips):
                level = self.level_of(sign * (gap - half * self.strips - lane_no), under)
                value = jnp.full((1, self.rows), self.cum[head, level], F32)
                values = value if values is None else jnp.where(self.lane_strip == lane_no, value, values)
            table.append(values)
        return jnp.concatenate(table, axis=1)

    def run(self, left, right, gap, side, diagonal=False, acc=None, banded=None):
        sign = 1 - 2 * side
        near = (self.row_at - self.lane_in) * sign >= 0
        for head in range(self.heads):
            cols = slice(head * self.depth, (head + 1) * self.depth)
            left_a, left_b = left(0, cols), left(1, cols)
            right_a, right_b = right(0, cols), right(1, cols)
            score = nt_dot(left_a, right_a)
            dweight = nt_dot(left_b, right_b)
            weights, dpres = [], []
            for strip in range(score.shape[0] // self.sub):
                part = slice(strip * self.sub, (strip + 1) * self.sub)
                bias = jnp.where(
                    near, self.table(head, gap + strip, sign, 0), self.table(head, gap + strip, sign, 1)
                )
                pre = score[part] * self.inv_root + bias
                bottom = 1.0 + jnp.exp2(jnp.maximum(pre, -87.0) * -1.4426950408889634)
                sig = pl.reciprocal(bottom, approx=True)
                sig = sig * (2.0 - bottom * sig)
                weight = pre * sig
                dpre = dweight[part] * (sig + weight * (1.0 - sig))
                if diagonal:
                    causal = (self.row_at + strip * self.sub - self.lane_at) * sign >= 0
                    weight = jnp.where(causal, weight, 0.0)
                    dpre = jnp.where(causal, dpre, 0.0)
                if acc is not None:
                    weights.append(weight.astype(BF16))
                    dpres.append(dpre.astype(BF16))
                if banded is None:
                    continue
                whole = jnp.sum(dpre.reshape(self.sub // 8, 8, self.span), axis=0)
                inner = jnp.sum(jnp.where(near, dpre, 0.0).reshape(self.sub // 8, 8, self.span), axis=0)
                for half in range(2):
                    lanes = slice(half * self.rows, (half + 1) * self.rows)
                    for under, amount in ((0, inner[:, lanes]), (1, (whole - inner)[:, lanes])):
                        level = self.level_of(sign * (gap + strip - half * self.strips), under)
                        self.rab[side, head, jnp.where(banded, level, self.bands)] += amount
            if acc is not None:
                weight = jnp.concatenate(weights, axis=0)
                dpre = jnp.concatenate(dpres, axis=0)
                acc[side, 0, :, cols] += jnp.dot(weight, right_b, preferred_element_type=F32)
                acc[side, 1, :, cols] += jnp.dot(dpre, right_a, preferred_element_type=F32)

    def band_row(self, out_ref, core, scale):
        strip_of = lax.broadcasted_iota(jnp.int32, (self.bands, self.rows), 1) // self.sub
        level = lax.broadcasted_iota(jnp.int32, (self.bands, 128), 0)
        lane = lax.broadcasted_iota(jnp.int32, (self.bands, 128), 1)
        result = jnp.zeros((self.bands, 128), F32)
        for head in range(self.heads):
            step_no = lane - (core * self.heads + head) * self.bands
            inside = (step_no >= 0) & (step_no < self.bands)
            for side in range(2):
                sums = jnp.sum(self.rab[side, head, : self.bands], axis=1)
                for strip in range(self.strips):
                    amount = jnp.sum(jnp.where(strip_of == strip, sums, 0.0), axis=1, keepdims=True)
                    band = level - strip if side == 0 else level + strip
                    result = result + jnp.where(inside & (band >= step_no), amount, 0.0)
        out_ref[...] = jnp.sum(result, axis=0, keepdims=True) * scale


def position(rows):
    index = lax.axis_index("seq")
    chip, core = index // 2, lax.rem(index, 2)
    mine = pl.ds(pl.multiple_of(core * rows, rows), rows)
    others = pl.ds(pl.multiple_of((1 - core) * rows, rows), rows)
    return chip, core, mine, others


def own_kernel(steps_ref, kv_ref, qd_ref, acc, rab, cum, *, blocks_of):
    chip, core, _, _ = position(kv_ref.shape[1] // 2)
    acc[...] = jnp.zeros_like(acc)
    rab[...] = jnp.zeros_like(rab)
    blocks = blocks_of(cum, rab)
    blocks.sum_steps(steps_ref, core)
    kv, qd = lambda n, cols: kv_ref[n, :, cols], lambda n, cols: qd_ref[n, :, cols]
    blocks.run(qd, kv, jnp.int32(0), 0, diagonal=True, acc=acc, banded=True)
    blocks.run(kv, qd, jnp.int32(0), 1, diagonal=True, acc=acc)


def middle_kernel(*refs, rounds, key_side, ends, blocks_of, scale):
    count = len(rounds)
    steps_ref, kv_ref, qd_ref, acc_in, rab_in = refs[:5]
    pieces = refs[5 : 5 + count]
    acc, band_ref, stack, copied, rab, cum, plan = refs[5 + count :]
    rows = kv_ref.shape[1] // 2
    chip, core, _, _ = position(rows)
    chips = lax.axis_size("seq") // 2
    copies = [
        pltpu.make_async_copy(piece, stack.at[unit], copied.at[unit]) for unit, piece in enumerate(pieces)
    ]
    for copy in copies:
        copy.start()
    acc[...] = acc_in[...]
    rab[...] = rab_in[...]
    blocks = blocks_of(cum, rab)
    blocks.sum_steps(steps_ref, core)
    for unit, one in enumerate(rounds):
        plan[unit, 0] = of_chip(one.origin, chip)
        plan[unit, 1] = of_chip([int(n in key_side.get(unit, ())) for n in range(chips)], chip)
    for copy in copies:
        copy.wait()
    per_chip = 2 * blocks.strips

    def step(unit, unused):
        origin = plan[unit, 0]
        other = lambda n, cols: stack[unit, n, :, cols]
        gap = (chip - origin) * per_chip

        @pl.when(origin < chip)
        def _():
            blocks.run(lambda n, cols: qd_ref[n, :, cols], other, gap, 0, acc=acc, banded=True)

        @pl.when(origin > chip)
        def _():
            wanted = plan[unit, 1] == 1
            blocks.run(lambda n, cols: kv_ref[n, :, cols], other, gap, 1, acc=acc, banded=wanted)

        return unused

    lax.fori_loop(0, count, step, 0)

    tables = [[ends.get(n, (0, 0, -1))[part] for n in range(chips)] for part in range(3)]
    queries_at, keys_at, part = [of_chip(table, chip) for table in tables]

    @pl.when(part >= 0)
    def _():
        place = pl.ds(pl.multiple_of(part * rows, rows), rows)
        blocks.run(
            lambda n, cols: stack[queries_at, n, place, cols],
            lambda n, cols: stack[keys_at, n, :, cols],
            (chips - 1) * per_chip + part * blocks.strips,
            0,
            banded=True,
        )

    blocks.band_row(band_ref, core, scale)


def last_kernel(
    steps_ref, len_ref, kv_ref, qd_ref, acc_in, gate_ref, *refs, rounds, blocks_of, scale, inv_root
):
    pieces, (keep_ref, give_ref, acc, rab, cum) = refs[: len(rounds)], refs[len(rounds) :]
    rows = kv_ref.shape[1] // 2
    chip, core, mine, others = position(rows)
    acc[...] = acc_in[...]
    blocks = blocks_of(cum, rab)
    blocks.sum_steps(steps_ref, core)
    for one, piece in zip(rounds, pieces):
        origin = of_chip(one.origin, chip)
        gap = (chip - origin) * 2 * blocks.strips
        other = lambda n, cols: piece[n, :, cols]

        @pl.when(origin < chip)
        def _():
            blocks.run(lambda n, cols: qd_ref[n, :, cols], other, gap, 0, acc=acc)

        @pl.when(origin > chip)
        def _():
            blocks.run(lambda n, cols: kv_ref[n, :, cols], other, gap, 1, acc=acc)

    for out_ref, place, whose in ((give_ref, others, 1 - core), (keep_ref, mine, core)):
        start = (2 * chip + whose) * rows
        live = start + lax.broadcasted_iota(jnp.int32, (rows, 1), 0) < len_ref[0]
        attended = jnp.where(live, acc[0, 0, place] * scale, 0.0)
        out_ref[0] = (attended * gate_ref[0, place].astype(F32)).astype(BF16)
        out_ref[1] = (acc[0, 1, place] * (scale * inv_root)).astype(BF16)
        out_ref[2] = (acc[1, 1, place] * (scale * inv_root)).astype(BF16)
        out_ref[3] = (acc[1, 0, place] * scale).astype(BF16)
        out_ref[4] = (attended * gate_ref[1, place].astype(F32)).astype(BF16)


def assemble_kernel(keep_ref, got_ref, *refs):
    outs, (buf, copied) = refs[:5], refs[5:]
    wide = keep_ref.shape[2]
    core = lax.rem(lax.axis_index("seq"), 2)
    for half in range(2):

        @pl.when(core == half)
        def _():
            buf[:, :, half * wide : (half + 1) * wide] = keep_ref[...]
            buf[:, :, (1 - half) * wide : (2 - half) * wide] = got_ref[...]

    copies = [pltpu.make_async_copy(buf.at[n], out.at[0], copied.at[n]) for n, out in enumerate(outs)]
    for copy in copies:
        copy.start()
    for copy in copies:
        copy.wait()


def rab_kernel(row_ref, rab_ref, *, total_len):
    heads, bands = rab_ref.shape
    row = row_ref[...] / total_len
    for head in range(heads):
        rab_ref[head : head + 1, :] = row[:, head * bands : (head + 1) * bands]


def sum_over(value, axis, size, flip=1):
    while flip < size:
        value = value + lax.ppermute(value, axis, [(n, n ^ flip) for n in range(size)])
        flip *= 2
    return value


def params(units, span, wide, **more):
    return dict(
        compiler_params=pltpu.CompilerParams(vmem_limit_bytes=VMEM_LIMIT),
        cost_estimate=pl.CostEstimate(
            flops=int(units * 8 * span * span * wide * 10),
            bytes_accessed=int((units + 2) * 4 * span * wide),
            transcendentals=0,
        ),
        **more,
    )


def body(queries, keys, values, gates, lengths, rab_steps, out_grad, dp_size, seq_size):
    rows, width = queries.shape[1:]
    heads, bands = rab_steps.shape
    total_len = rows * seq_size
    chips = seq_size // 2
    span, wide, depth = 2 * rows, width // 2, width // heads
    inv_root, scale = depth**-0.5, total_len**-0.5
    blocks_of = functools.partial(
        Blocks, span=span, depth=depth, heads=heads // 2, bands=bands, band_width=total_len // bands, inv_root=inv_root
    )

    def send(value, route):
        pairs = [(2 * n + core, 2 * target + core) for n, target in route.items() for core in range(2)]
        return lax.ppermute(value, "seq", pairs)

    across_chip = [(n, n ^ 1) for n in range(seq_size)]
    packed = jax.ShapeDtypeStruct((6, rows, wide), BF16)
    same, cross = pl.pallas_call(
        prep_kernel,
        out_shape=(packed, packed),
        in_specs=[SMEM] + [HBM] * 5,
        out_specs=(VMEM,) * 2,
        scratch_shapes=[pltpu.VMEM((5, rows, width), BF16), pltpu.SemaphoreType.DMA((5,))],
        compiler_params=pltpu.CompilerParams(vmem_limit_bytes=PREP_LIMIT),
        name="prep",
    )(lengths, keys, values, queries, gates, out_grad)
    own = jax.ShapeDtypeStruct((2, span, wide), BF16)
    own_kv, own_qd, gate, low, even = pl.pallas_call(
        functools.partial(build_kernel, chips=chips),
        out_shape=(own,) * 5,
        in_specs=[VMEM] * 2,
        out_specs=(VMEM,) * 5,
        compiler_params=pltpu.CompilerParams(vmem_limit_bytes=VMEM_LIMIT),
        name="build",
    )(same, lax.ppermute(cross, "seq", across_chip))

    early, late, key_side, ends = plan_rounds(chips)
    ready = {"kv": own_kv, "qd": own_qd, "low": low, "even": even}
    got = [send(ready[one.payload], one.route) if isinstance(one.payload, str) else None for one in early]

    acc = jax.ShapeDtypeStruct((2, 2, span, wide), F32)
    rab = jax.ShapeDtypeStruct((2, heads // 2, bands + 1, 8, rows), F32)
    cum = pltpu.SMEM((heads // 2, bands), F32)
    acc_now, rab_now = pl.pallas_call(
        functools.partial(own_kernel, blocks_of=blocks_of),
        out_shape=(acc, rab),
        in_specs=[SMEM, VMEM, VMEM],
        out_specs=(VMEM,) * 2,
        scratch_shapes=[cum],
        **params(2, span, wide, name="attend_own"),
    )(rab_steps, own_kv, own_qd)

    acc_now, got[0] = lax.optimization_barrier((acc_now, got[0]))
    for n, one in enumerate(early):
        if got[n] is None:
            got[n] = send(got[one.payload], one.route)
    ahead = send(got[late[0].payload], late[0].route)
    acc_now, row = pl.pallas_call(
        functools.partial(
            middle_kernel, rounds=early, key_side=key_side, ends=ends, blocks_of=blocks_of, scale=scale
        ),
        out_shape=(acc, jax.ShapeDtypeStruct((1, 128), F32)),
        in_specs=[SMEM] + [VMEM] * 4 + [ANY] * len(got),
        out_specs=(VMEM,) * 2,
        scratch_shapes=[
            pltpu.VMEM((len(early), 2, span, wide), BF16),
            pltpu.SemaphoreType.DMA((len(early),)),
            pltpu.VMEM(rab.shape, F32),
            cum,
            pltpu.SMEM((len(early), 2), jnp.int32),
        ],
        **params(len(early), span, wide, name="attend_middle"),
    )(rab_steps, own_kv, own_qd, acc_now, rab_now, *got)

    acc_now, ahead, *kept = lax.optimization_barrier((acc_now, ahead, *[got[one.payload] for one in late[1:]]))
    tail = [ahead] + [send(value, one.route) for value, one in zip(kept, late[1:])]
    row = row + lax.ppermute(row, "seq", across_chip)
    row = sum_over(row, "dp", dp_size)
    row, tail = lax.optimization_barrier((row, tail))
    row = row + lax.ppermute(row, "seq", [(n, n ^ 2) for n in range(seq_size)])
    half_out = jax.ShapeDtypeStruct((5, rows, wide), BF16)
    keep, give = pl.pallas_call(
        functools.partial(last_kernel, rounds=late, blocks_of=blocks_of, scale=scale, inv_root=inv_root),
        out_shape=(half_out, half_out),
        in_specs=[SMEM, SMEM] + [VMEM] * (4 + len(tail)),
        out_specs=(VMEM,) * 2,
        scratch_shapes=[pltpu.VMEM(acc.shape, F32), pltpu.VMEM(rab.shape, F32), cum],
        **params(len(late), span, wide, name="attend_last"),
    )(rab_steps, lengths, own_kv, own_qd, acc_now, gate, *tail)
    row, give = lax.optimization_barrier((row, give))
    row = sum_over(row, "seq", seq_size, 4)
    theirs = lax.ppermute(give, "seq", across_chip)
    out = jax.ShapeDtypeStruct(queries.shape, BF16)
    outs = pl.pallas_call(
        assemble_kernel,
        out_shape=(out,) * 5,
        in_specs=[VMEM] * 2,
        out_specs=(HBM,) * 5,
        scratch_shapes=[pltpu.VMEM((5, rows, width), BF16), pltpu.SemaphoreType.DMA((5,))],
        compiler_params=pltpu.CompilerParams(vmem_limit_bytes=VMEM_LIMIT),
        name="assemble",
    )(keep, theirs)
    rab_grad = pl.pallas_call(
        functools.partial(rab_kernel, total_len=total_len),
        out_shape=jax.ShapeDtypeStruct((heads, bands), F32),
        in_specs=[VMEM],
        out_specs=VMEM,
        name="bias_grad",
    )(row)
    return (*outs, rab_grad)


def solution(mesh):
    rows = P("dp", "seq", None)
    return jax.shard_map(
        functools.partial(body, dp_size=mesh.shape["dp"], seq_size=mesh.shape["seq"]),
        mesh=mesh,
        in_specs=(rows, rows, rows, rows, P("dp"), P(), rows),
        out_specs=(rows, rows, rows, rows, rows, P()),
        check_vma=False,
    )
```

time: 54.5 us -> 48.3 us (0.89)
  starting transfers between devices: 22.1 us -> 17.7 us
  Pallas kernels: 11.8 us -> 10.4 us
  local copies, waits for them, and re-layouts: 1.82 us -> 1 us
  waiting for transfers between devices: 16.4 us -> 17 us
    ppermute x0 -> x7, starting transfers between devices: none -> 8.99 us  [the longest x3 6.12 us: sum_over(): lax.ppermute(value, axis, [(n, n ^ flip) for n in range(size)])]
    ppermute x0 -> x7, waiting for transfers between devices: none -> 8.34 us  [the longest x3 5.66 us: sum_over(): lax.ppermute(value, axis, [(n, n ^ flip) for n in range(size)])]
    ppermute x10 -> x5, waiting for transfers between devices: 16.4 us -> 8.66 us  [send(): return lax.ppermute(value, 'seq', pairs)]
    ppermute x10 -> x5, starting transfers between devices: 15.4 us -> 8.67 us  [send(): return lax.ppermute(value, 'seq', pairs)]
    all_to_all x1 -> x0, starting transfers between devices: 6.66 us -> none  [body(): band = lax.all_to_all(band, ('dp', 'seq') if together else 'seq', 0, 0)]
    pallas_call x5 -> x7, Pallas kernels: 11.8 us -> 10.4 us  [the longest x1 2.24 us: body(): pl.pallas_call(functools.partial(last_kernel, rounds=late, blocks_of=bloc...]
    unnamed x10 -> x4, local copies, waits for them, and re-layouts: 1.82 us -> 1 us
    div x1 -> x0, other arithmetic: 0.58 us -> none  [body(): return (*outs, band[:heads, :bands] / total_len)]
  transfers between devices with their start and end apart: 11 -> 12, of which waited for: 5 -> 9; matrix products, arithmetic and copies ran while one was open for 1% -> 1% of each run, Pallas kernels for 5% -> 15%
where the time goes in v2:
time: 48.3 us; the launch traced here: 48 us
  starting transfers between devices  17.7 us (37%)
  waiting for transfers between devices  17 us (35%)
  Pallas kernels  10.4 us (22%)
  between operations  1.4 us (3%)
  local copies, waits for them, and re-layouts  1 us (2%)
  other arithmetic  0.53 us (1%)
    ppermute x5, starting transfers between devices, send(): return lax.ppermute(value, 'seq', pairs)  8.67 us
    ppermute x5, waiting for transfers between devices, send(): return lax.ppermute(value, 'seq', pairs)  8.66 us
    ppermute x3, starting transfers between devices, sum_over(): lax.ppermute(value, axis, [(n, n ^ flip) for n in range(size)])  6.12 us
    ppermute x3, waiting for transfers between devices, sum_over(): lax.ppermute(value, axis, [(n, n ^ flip) for n in range(size)])  5.66 us
    pallas_call x1, Pallas kernels, body(): pl.pallas_call(functools.partial(last_kernel, rounds=late, blocks_of=bloc...  2.24 us
    ppermute x1, starting transfers between devices, body(): row = row + lax.ppermute(row, 'seq', [(n, n ^ 2) for n in range(seq_size)])  2.21 us
    pallas_call x1, Pallas kernels, body(): pl.pallas_call(prep_kernel, out_shape=(packed, packed), in_specs=[SMEM] +...  2.18 us
    pallas_call x1, Pallas kernels, body(): pl.pallas_call(functools.partial(own_kernel, blocks_of=blocks_of), out_sh...  1.88 us
  transfers between devices with their start and end apart: 12, of which 9 were waited for; matrix products, arithmetic and copies ran while one was open for 1% of the time, Pallas kernels for 15%

profile of v2, /device:TPU:0, one launch (start us, length us, event | category | flops | bytes accessed | tf_op | source)
XLA Modules:
  0.0 48.0 jit_solution(12048740542174865311)
XLA Ops:
  1.3 2.2 %prep.1 = (bf16[6,128,256]{2,1,0:T(8,128)(2,1)}, bf16[6,128,256]{2,1,0:T(8,128)(2,1)}) custom-call(s32[1]{0:T(128)S(6)} %copy.13.len_ref, bf16[1,128,512]{2,1,0:T(8,128)(2,1)} %k_ref.1, bf16[1,128,512]{2,1,0:T(8,128)(2,1)} %v_ref.1, bf16[1,128,512]{2,1,0:T(8,128)(2,1)} %q_ref.1, bf16[1,128,512]{2,1,0:T(8,128)(2,1)} %u_ref.1, bf16[1,128,512]{2,1,0:T(8,128)(2,1)} %og_ref.1), custom_call_target="tpu_custom_call" | custom-call | tf_op jit(solution)/shard_map/prep/pallas_call | solution.py:383
  3.5 0.5 %collective-permute-start = (bf16[6,128,256]{2,1,0:T(8,128)(2,1)}, bf16[6,128,256]{2,1,0:T(8,128)(2,1)S(1)}, u32[]{:S(2)}, u32[]{:S(2)}) collective-permute-start(bf16[6,128,256]{2,1,0:T(8,128)(2,1)} %get-tuple-element.35), channel_id=1, source_target_pairs={{0,1},{1,0},{2,3},{3,2},{4,5},{5,4},{6,7},{7,6},{8,9},{9,8},{10,11... | collective-permute-start | bytes 1179656 | tf_op jit(solution)/shard_map/ppermute | solution.py:400
  4.0 1.6 %collective-permute-done.near_ref = bf16[6,128,256]{2,1,0:T(8,128)(2,1)S(1)} collective-permute-done((bf16[6,128,256]{2,1,0:T(8,128)(2,1)}, bf16[6,128,256]{2,1,0:T(8,128)(2,1)S(1)}, u32[]{:S(2)}, u32[]{:S(2)}) %collective-permute-start) | collective-permute-done | bytes 393248 | tf_op jit(solution)/shard_map/ppermute | solution.py:400
  5.5 1.0 %copy-done = bf16[6,128,256]{2,1,0:T(8,128)(2,1)S(1)} copy-done((bf16[6,128,256]{2,1,0:T(8,128)(2,1)S(1)}, bf16[6,128,256]{2,1,0:T(8,128)(2,1)}, u32[]{:S(2)}) %copy-start) | copy-done | bytes 393240
  6.5 0.1 build.1
  6.7 4.0 %collective-permute-start.1 = (bf16[2,256,256]{2,1,0:T(8,128)(2,1)S(1)}, bf16[2,256,256]{2,1,0:T(8,128)(2,1)S(1)}, u32[]{:S(2)}, u32[]{:S(2)}) collective-permute-start(bf16[2,256,256]{2,1,0:T(8,128)(2,1)S(1)} %get-tuple-element.39), channel_id=1, source_target_pairs={{0,4},{1,5},{6,2},{7,3},{2,0},{3,1},{4,6},{5,7},{8,12},{9,13},{14,... | collective-permute-start | bytes 786440 | tf_op jit(solution)/shard_map/ppermute | solution.py:379
  10.7 1.4 %collective-permute-start.3 = (bf16[2,256,256]{2,1,0:T(8,128)(2,1)S(1)}, bf16[2,256,256]{2,1,0:T(8,128)(2,1)S(1)}, u32[]{:S(2)}, u32[]{:S(2)}) collective-permute-start(bf16[2,256,256]{2,1,0:T(8,128)(2,1)S(1)} %get-tuple-element.43), channel_id=1, source_target_pairs={{0,2},{1,3},{6,4},{7,5},{8,10},{9,11},{14,12},{15,13},{16,18},{17,... | collective-permute-start | bytes 786440 | tf_op jit(solution)/shard_map/ppermute | solution.py:379
  12.1 0.7 %collective-permute-start.2 = (bf16[2,256,256]{2,1,0:T(8,128)(2,1)S(1)}, bf16[2,256,256]{2,1,0:T(8,128)(2,1)S(1)}, u32[]{:S(2)}, u32[]{:S(2)}) collective-permute-start(bf16[2,256,256]{2,1,0:T(8,128)(2,1)S(1)} %get-tuple-element.43), channel_id=1, source_target_pairs={{2,4},{3,5},{4,2},{5,3},{10,12},{11,13},{12,10},{13,11},{18,20},{1... | collective-permute-start | bytes 786440 | tf_op jit(solution)/shard_map/ppermute | solution.py:379
  12.8 1.9 %attend_own.1 = (f32[2,2,256,256]{3,2,1,0:T(8,128)S(1)}, f32[2,2,17,8,128]{4,3,2,1,0:T(8,128)S(1)}) custom-call(f32[4,16]{1,0:T(4,128)S(1)} %copy-done.1, bf16[2,256,256]{2,1,0:T(8,128)(2,1)S(1)} %get-tuple-element.36.kv_ref.refs_1_, bf16[2,256,256]{2,1,0:T(8,128)(2,1)S(1)} %get-tuple-element.37.qd_ref.refs_2_), custom_call_target="tpu_custom_call" | custom-call | flops 2684354560 | bytes 1048576 | tf_op jit(solution)/shard_map/attend_own/pallas_call | solution.py:409
  14.7 2.6 %collective-permute-done.1.refs_5_ = bf16[2,256,256]{2,1,0:T(8,128)(2,1)S(1)} collective-permute-done((bf16[2,256,256]{2,1,0:T(8,128)(2,1)S(1)}, bf16[2,256,256]{2,1,0:T(8,128)(2,1)S(1)}, u32[]{:S(2)}, u32[]{:S(2)}) %collective-permute-start.1) | collective-permute-done | bytes 262176 | tf_op jit(solution)/shard_map/ppermute | solution.py:379
  17.3 1.3 %collective-permute-start.4 = (bf16[2,256,256]{2,1,0:T(8,128)(2,1)S(1)}, bf16[2,256,256]{2,1,0:T(8,128)(2,1)S(1)}, u32[]{:S(2)}, u32[]{:S(2)}) collective-permute-start(bf16[2,256,256]{2,1,0:T(8,128)(2,1)S(1)} %collective-permute-done.1.refs_5_), channel_id=1, source_target_pairs={{4,6},{5,7},{2,0},{3,1},{12,14},{13,15},{10,8},{11,9},{20,22},{21,... | collective-permute-start | bytes 786440 | tf_op jit(solution)/shard_map/ppermute | solution.py:379
  18.6 3.5 %collective-permute-done.3.refs_7_ = bf16[2,256,256]{2,1,0:T(8,128)(2,1)S(1)} collective-permute-done((bf16[2,256,256]{2,1,0:T(8,128)(2,1)S(1)}, bf16[2,256,256]{2,1,0:T(8,128)(2,1)S(1)}, u32[]{:S(2)}, u32[]{:S(2)}) %collective-permute-start.3) | collective-permute-done | bytes 262176 | tf_op jit(solution)/shard_map/ppermute | solution.py:379
  22.1 0.0 collective-permute-done.2.refs_6_
  22.2 1.8 %attend_middle.1 = (f32[2,2,256,256]{3,2,1,0:T(8,128)S(1)}, f32[1,128]{1,0:T(1,128)S(1)}) custom-call(f32[4,16]{1,0:T(4,128)S(1)} %copy-done.1, bf16[2,256,256]{2,1,0:T(8,128)(2,1)S(1)} %get-tuple-element.36.kv_ref.refs_1_, bf16[2,256,256]{2,1,0:T(8,128)(2,1)S(1)} %get-tuple-element.37.qd_ref.refs_2_, f32[2,2,256,256]{3,2,1,0:T(8,128)S(1)} %get-tuple-element.40.refs_3_, ...), custom_call_target="tpu_custom_call" | custom-call | flops 4026531840 | bytes 1310720 | tf_op jit(solution)/shard_map/attend_middle/pallas_call | solution.py:423
  24.0 2.0 %collective-permute-done.4.refs_0_ = bf16[2,256,256]{2,1,0:T(8,128)(2,1)S(1)} collective-permute-done((bf16[2,256,256]{2,1,0:T(8,128)(2,1)S(1)}, bf16[2,256,256]{2,1,0:T(8,128)(2,1)S(1)}, u32[]{:S(2)}, u32[]{:S(2)}) %collective-permute-start.4) | collective-permute-done | bytes 262176 | tf_op jit(solution)/shard_map/ppermute | solution.py:379
  26.0 1.3 %collective-permute-start.8 = (bf16[2,256,256]{2,1,0:T(8,128)(2,1)S(1)}, bf16[2,256,256]{2,1,0:T(8,128)(2,1)S(1)}, u32[]{:S(2)}, u32[]{:S(2)}) collective-permute-start(bf16[2,256,256]{2,1,0:T(8,128)(2,1)S(1)} %collective-permute-done.2.refs_6_), channel_id=1, source_target_pairs={{4,6},{5,7},{2,0},{3,1},{12,14},{13,15},{10,8},{11,9},{20,22},{21,... | collective-permute-start | bytes 786440 | tf_op jit(solution)/shard_map/ppermute | solution.py:379
  27.3 0.1 collective-permute-start.5
  27.4 1.1 %collective-permute-done.5 = f32[1,128]{1,0:T(1,128)S(1)} collective-permute-done((f32[1,128]{1,0:T(1,128)S(1)}, f32[1,128]{1,0:T(1,128)S(1)}, u32[]{:S(2)}, u32[]{:S(2)}) %collective-permute-start.5) | collective-permute-done | bytes 544 | tf_op jit(solution)/shard_map/ppermute | solution.py:442
  28.5 1.5 %collective-permute-start.6 = (f32[1,128]{1,0:T(1,128)S(1)}, f32[1,128]{1,0:T(1,128)S(1)}, u32[]{:S(2)}, u32[]{:S(2)}) collective-permute-start(f32[1,128]{1,0:T(1,128)S(1)} %add.15), channel_id=1, source_target_pairs={{0,8},{8,0},{16,24},{24,16},{1,9},{9,1},{17,25},{25,17},{2,10},{10... | collective-permute-start | bytes 1544 | tf_op jit(solution)/shard_map/ppermute | solution.py:349
  29.9 2.1 %collective-permute-done.6 = f32[1,128]{1,0:T(1,128)S(1)} collective-permute-done((f32[1,128]{1,0:T(1,128)S(1)}, f32[1,128]{1,0:T(1,128)S(1)}, u32[]{:S(2)}, u32[]{:S(2)}) %collective-permute-start.6) | collective-permute-done | bytes 544 | tf_op jit(solution)/shard_map/ppermute | solution.py:349
  32.0 1.5 %collective-permute-start.7 = (f32[1,128]{1,0:T(1,128)S(1)}, f32[1,128]{1,0:T(1,128)S(1)}, u32[]{:S(2)}, u32[]{:S(2)}) collective-permute-start(f32[1,128]{1,0:T(1,128)S(1)} %add.16), channel_id=1, source_target_pairs={{0,16},{8,24},{16,0},{24,8},{1,17},{9,25},{17,1},{25,9},{2,18},{10... | collective-permute-start | bytes 1544 | tf_op jit(solution)/shard_map/ppermute | solution.py:349
  33.5 2.1 %collective-permute-done.7 = f32[1,128]{1,0:T(1,128)S(1)} collective-permute-done((f32[1,128]{1,0:T(1,128)S(1)}, f32[1,128]{1,0:T(1,128)S(1)}, u32[]{:S(2)}, u32[]{:S(2)}) %collective-permute-start.7) | collective-permute-done | bytes 544 | tf_op jit(solution)/shard_map/ppermute | solution.py:349
  35.6 0.4 collective-permute-done.8.refs_1_
  36.0 2.2 %collective-permute-start.9 = (f32[1,128]{1,0:T(1,128)S(1)}, f32[1,128]{1,0:T(1,128)S(1)}, u32[]{:S(2)}, u32[]{:S(2)}) collective-permute-start(f32[1,128]{1,0:T(1,128)S(1)} %add.17), channel_id=1, source_target_pairs={{0,2},{1,3},{2,0},{3,1},{4,6},{5,7},{6,4},{7,5},{8,10},{9,11},{10,... | collective-permute-start | bytes 1544 | tf_op jit(solution)/shard_map/ppermute | solution.py:445
  38.2 2.2 %attend_last.1 = (bf16[5,128,256]{2,1,0:T(8,128)(2,1)S(1)}, bf16[5,128,256]{2,1,0:T(8,128)(2,1)S(1)}) custom-call(f32[4,16]{1,0:T(4,128)S(1)} %copy-done.1, s32[1]{0:T(128)S(6)} %copy.13.len_ref, bf16[2,256,256]{2,1,0:T(8,128)(2,1)S(1)} %get-tuple-element.36.kv_ref.refs_1_, bf16[2,256,256]{2,1,0:T(8,128)(2,1)S(1)} %get-tuple-element.37.qd_ref.refs_2_, ...), custom_call_target="tpu_custom_call" | custom-call | flops 2684354560 | bytes 1048576 | tf_op jit(solution)/shard_map/attend_last/pallas_call | solution.py:447
  40.5 0.0 collective-permute-done.9
  40.5 0.1 collective-permute-start.10
  40.6 3.2 %collective-permute-start.11 = (f32[1,128]{1,0:T(1,128)S(1)}, f32[1,128]{1,0:T(1,128)S(1)}, u32[]{:S(2)}, u32[]{:S(2)}) collective-permute-start(f32[1,128]{1,0:T(1,128)S(1)} %add.18), channel_id=1, source_target_pairs={{0,4},{1,5},{2,6},{3,7},{4,0},{5,1},{6,2},{7,3},{8,12},{9,13},{10,... | collective-permute-start | bytes 1544 | tf_op jit(solution)/shard_map/ppermute | solution.py:349
  43.7 1.5 %collective-permute-done.11 = f32[1,128]{1,0:T(1,128)S(1)} collective-permute-done((f32[1,128]{1,0:T(1,128)S(1)}, f32[1,128]{1,0:T(1,128)S(1)}, u32[]{:S(2)}, u32[]{:S(2)}) %collective-permute-start.11) | collective-permute-done | bytes 544 | tf_op jit(solution)/shard_map/ppermute | solution.py:349
  45.3 0.5 %add.19.row_ref = f32[1,128]{1,0:T(1,128)} add(f32[1,128]{1,0:T(1,128)S(1)} %add.18, f32[1,128]{1,0:T(1,128)S(1)} %collective-permute-done.11) | non-fusion elementwise | flops 128 | bytes 1536 | tf_op jit(solution)/shard_map/add | solution.py:349
  45.8 1.3 %bias_grad.1 = f32[4,16]{1,0:T(4,128)} custom-call(f32[1,128]{1,0:T(1,128)} %add.19.row_ref), custom_call_target="tpu_custom_call" | custom-call | tf_op jit(solution)/shard_map/bias_grad/pallas_call | solution.py:468
  47.1 0.9 %assemble.1 = (bf16[1,128,512]{2,1,0:T(8,128)(2,1)}, bf16[1,128,512]{2,1,0:T(8,128)(2,1)}, bf16[1,128,512]{2,1,0:T(8,128)(2,1)}, bf16[1,128,512]{2,1,0:T(8,128)(2,1)}, bf16[1,128,512]{2,1,0:T(8,128)(2,1)}) custom-call(bf16[5,128,256]{2,1,0:T(8,128)(2,1)S(1)} %get-tuple-element.52.keep_ref, bf16[5,128,256]{2,1,0:T(8,128)(2,1)S(1)} %collective-permute-done.10.got_ref), custom_call_target="tpu_custom_call" | custom-call | tf_op jit(solution)/shard_map/assemble/pallas_call | solution.py:459
  (8 shorter events, 0.0 us)
Async XLA Ops:
  3.5 2.1 %collective-permute-start = (bf16[6,128,256]{2,1,0:T(8,128)(2,1)}, bf16[6,128,256]{2,1,0:T(8,128)(2,1)S(1)}, u32[]{:S(2)}, u32[]{:S(2)}) collective-permute-start(bf16[6,128,256]{2,1,0:T(8,128)(2,1)} %get-tuple-element.35), channel_id=1, source_target_pairs={{0,1},{1,0},{2,3},{3,2},{4,5},{5,4},{6,7},{7,6},{8,9},{9,8},{10,11... | collective-permute-start | bytes 1179656 | tf_op jit(solution)/shard_map/ppermute | solution.py:400
  5.5 1.0 %copy-start = (bf16[6,128,256]{2,1,0:T(8,128)(2,1)S(1)}, bf16[6,128,256]{2,1,0:T(8,128)(2,1)}, u32[]{:S(2)}) copy-start(bf16[6,128,256]{2,1,0:T(8,128)(2,1)} %get-tuple-element.34.same_ref) | copy-start | bytes 1179652
  6.7 10.7 %collective-permute-start.1 = (bf16[2,256,256]{2,1,0:T(8,128)(2,1)S(1)}, bf16[2,256,256]{2,1,0:T(8,128)(2,1)S(1)}, u32[]{:S(2)}, u32[]{:S(2)}) collective-permute-start(bf16[2,256,256]{2,1,0:T(8,128)(2,1)S(1)} %get-tuple-element.39), channel_id=1, source_target_pairs={{0,4},{1,5},{6,2},{7,3},{2,0},{3,1},{4,6},{5,7},{8,12},{9,13},{14,... | collective-permute-start | bytes 786440 | tf_op jit(solution)/shard_map/ppermute | solution.py:379
  10.7 2.1 %copy-start.1 = (f32[4,16]{1,0:T(4,128)S(1)}, f32[4,16]{1,0:T(4,128)}, u32[]{:S(2)}) copy-start(f32[4,16]{1,0:T(4,128)} %steps_ref.3) | copy-start | bytes 772
  10.7 11.5 %collective-permute-start.3 = (bf16[2,256,256]{2,1,0:T(8,128)(2,1)S(1)}, bf16[2,256,256]{2,1,0:T(8,128)(2,1)S(1)}, u32[]{:S(2)}, u32[]{:S(2)}) collective-permute-start(bf16[2,256,256]{2,1,0:T(8,128)(2,1)S(1)} %get-tuple-element.43), channel_id=1, source_target_pairs={{0,2},{1,3},{6,4},{7,5},{8,10},{9,11},{14,12},{15,13},{16,18},{17,... | collective-permute-start | bytes 786440 | tf_op jit(solution)/shard_map/ppermute | solution.py:379
  12.1 10.1 %collective-permute-start.2 = (bf16[2,256,256]{2,1,0:T(8,128)(2,1)S(1)}, bf16[2,256,256]{2,1,0:T(8,128)(2,1)S(1)}, u32[]{:S(2)}, u32[]{:S(2)}) collective-permute-start(bf16[2,256,256]{2,1,0:T(8,128)(2,1)S(1)} %get-tuple-element.43), channel_id=1, source_target_pairs={{2,4},{3,5},{4,2},{5,3},{10,12},{11,13},{12,10},{13,11},{18,20},{1... | collective-permute-start | bytes 786440 | tf_op jit(solution)/shard_map/ppermute | solution.py:379
  17.3 8.7 %collective-permute-start.4 = (bf16[2,256,256]{2,1,0:T(8,128)(2,1)S(1)}, bf16[2,256,256]{2,1,0:T(8,128)(2,1)S(1)}, u32[]{:S(2)}, u32[]{:S(2)}) collective-permute-start(bf16[2,256,256]{2,1,0:T(8,128)(2,1)S(1)} %collective-permute-done.1.refs_5_), channel_id=1, source_target_pairs={{4,6},{5,7},{2,0},{3,1},{12,14},{13,15},{10,8},{11,9},{20,22},{21,... | collective-permute-start | bytes 786440 | tf_op jit(solution)/shard_map/ppermute | solution.py:379
  26.0 10.0 %collective-permute-start.8 = (bf16[2,256,256]{2,1,0:T(8,128)(2,1)S(1)}, bf16[2,256,256]{2,1,0:T(8,128)(2,1)S(1)}, u32[]{:S(2)}, u32[]{:S(2)}) collective-permute-start(bf16[2,256,256]{2,1,0:T(8,128)(2,1)S(1)} %collective-permute-done.2.refs_6_), channel_id=1, source_target_pairs={{4,6},{5,7},{2,0},{3,1},{12,14},{13,15},{10,8},{11,9},{20,22},{21,... | collective-permute-start | bytes 786440 | tf_op jit(solution)/shard_map/ppermute | solution.py:379
  27.3 1.2 %collective-permute-start.5 = (f32[1,128]{1,0:T(1,128)S(1)}, f32[1,128]{1,0:T(1,128)S(1)}, u32[]{:S(2)}, u32[]{:S(2)}) collective-permute-start(f32[1,128]{1,0:T(1,128)S(1)} %get-tuple-element.47), channel_id=1, source_target_pairs={{0,1},{1,0},{2,3},{3,2},{4,5},{5,4},{6,7},{7,6},{8,9},{9,8},{10,11... | collective-permute-start | bytes 1544 | tf_op jit(solution)/shard_map/ppermute | solution.py:442
  28.5 3.5 %collective-permute-start.6 = (f32[1,128]{1,0:T(1,128)S(1)}, f32[1,128]{1,0:T(1,128)S(1)}, u32[]{:S(2)}, u32[]{:S(2)}) collective-permute-start(f32[1,128]{1,0:T(1,128)S(1)} %add.15), channel_id=1, source_target_pairs={{0,8},{8,0},{16,24},{24,16},{1,9},{9,1},{17,25},{25,17},{2,10},{10... | collective-permute-start | bytes 1544 | tf_op jit(solution)/shard_map/ppermute | solution.py:349
  32.0 3.5 %collective-permute-start.7 = (f32[1,128]{1,0:T(1,128)S(1)}, f32[1,128]{1,0:T(1,128)S(1)}, u32[]{:S(2)}, u32[]{:S(2)}) collective-permute-start(f32[1,128]{1,0:T(1,128)S(1)} %add.16), channel_id=1, source_target_pairs={{0,16},{8,24},{16,0},{24,8},{1,17},{9,25},{17,1},{25,9},{2,18},{10... | collective-permute-start | bytes 1544 | tf_op jit(solution)/shard_map/ppermute | solution.py:349
  36.0 4.5 %collective-permute-start.9 = (f32[1,128]{1,0:T(1,128)S(1)}, f32[1,128]{1,0:T(1,128)S(1)}, u32[]{:S(2)}, u32[]{:S(2)}) collective-permute-start(f32[1,128]{1,0:T(1,128)S(1)} %add.17), channel_id=1, source_target_pairs={{0,2},{1,3},{2,0},{3,1},{4,6},{5,7},{6,4},{7,5},{8,10},{9,11},{10,... | collective-permute-start | bytes 1544 | tf_op jit(solution)/shard_map/ppermute | solution.py:445
  40.5 6.6 %collective-permute-start.10 = (bf16[5,128,256]{2,1,0:T(8,128)(2,1)S(1)}, bf16[5,128,256]{2,1,0:T(8,128)(2,1)S(1)}, u32[]{:S(2)}, u32[]{:S(2)}) collective-permute-start(bf16[5,128,256]{2,1,0:T(8,128)(2,1)S(1)} %get-tuple-element.55), channel_id=1, source_target_pairs={{0,1},{1,0},{2,3},{3,2},{4,5},{5,4},{6,7},{7,6},{8,9},{9,8},{10,11... | collective-permute-start | bytes 983048 | tf_op jit(solution)/shard_map/ppermute | solution.py:457
  40.6 4.7 %collective-permute-start.11 = (f32[1,128]{1,0:T(1,128)S(1)}, f32[1,128]{1,0:T(1,128)S(1)}, u32[]{:S(2)}, u32[]{:S(2)}) collective-permute-start(f32[1,128]{1,0:T(1,128)S(1)} %add.18), channel_id=1, source_target_pairs={{0,4},{1,5},{2,6},{3,7},{4,0},{5,1},{6,2},{7,3},{8,12},{9,13},{10,... | collective-permute-start | bytes 1544 | tf_op jit(solution)/shard_map/ppermute | solution.py:349

commit v3 on v2

--- a/solution.py
+++ b/solution.py
@@ -205,7 +205,8 @@
                     amount = jnp.sum(jnp.where(strip_of == strip, sums, 0.0), axis=1, keepdims=True)
                     band = level - strip if side == 0 else level + strip
                     result = result + jnp.where(inside & (band >= step_no), amount, 0.0)
-        out_ref[...] = jnp.sum(result, axis=0, keepdims=True) * scale
+        row = jnp.sum(result, axis=0, keepdims=True) * scale
+        out_ref[...] = jnp.broadcast_to(row[None], out_ref.shape)
 
 
 def position(rows):
@@ -227,11 +228,14 @@
     blocks.run(kv, qd, jnp.int32(0), 1, diagonal=True, acc=acc)
 
 
-def middle_kernel(*refs, rounds, key_side, ends, blocks_of, scale):
+def middle_kernel(*refs, rounds, done, key_side, ends, blocks_of, scale):
     count = len(rounds)
     steps_ref, kv_ref, qd_ref, acc_in, rab_in = refs[:5]
     pieces = refs[5 : 5 + count]
-    acc, band_ref, stack, copied, rab, cum, plan = refs[5 + count :]
+    if ends is None:
+        acc, rab, stack, copied, cum, plan = refs[5 + count :]
+    else:
+        acc, band_ref, stack, copied, cum, plan, rab = refs[5 + count :]
     rows = kv_ref.shape[1] // 2
     chip, core, _, _ = position(rows)
     chips = lax.axis_size("seq") // 2
@@ -267,7 +271,9 @@
 
         return unused
 
-    lax.fori_loop(0, count, step, 0)
+    lax.fori_loop(done, count, step, 0)
+    if ends is None:
+        return
 
     tables = [[ends.get(n, (0, 0, -1))[part] for n in range(chips)] for part in range(3)]
     queries_at, keys_at, part = [of_chip(table, chip) for table in tables]
@@ -286,14 +292,11 @@
     blocks.band_row(band_ref, core, scale)
 
 
-def last_kernel(
-    steps_ref, len_ref, kv_ref, qd_ref, acc_in, gate_ref, *refs, rounds, blocks_of, scale, inv_root
-):
-    pieces, (keep_ref, give_ref, acc, rab, cum) = refs[: len(rounds)], refs[len(rounds) :]
-    rows = kv_ref.shape[1] // 2
-    chip, core, mine, others = position(rows)
+def late_kernel(steps_ref, kv_ref, qd_ref, acc_in, *refs, rounds, blocks_of):
+    pieces, (acc, cum) = refs[: len(rounds)], refs[len(rounds) :]
+    chip, core, _, _ = position(kv_ref.shape[1] // 2)
     acc[...] = acc_in[...]
-    blocks = blocks_of(cum, rab)
+    blocks = blocks_of(cum, None)
     blocks.sum_steps(steps_ref, core)
     for one, piece in zip(rounds, pieces):
         origin = of_chip(one.origin, chip)
@@ -308,6 +311,10 @@
         def _():
             blocks.run(lambda n, cols: kv_ref[n, :, cols], other, gap, 1, acc=acc)
 
+
+def results_kernel(len_ref, acc, gate_ref, keep_ref, give_ref, *, scale, inv_root):
+    rows = keep_ref.shape[1]
+    chip, core, mine, others = position(rows)
     for out_ref, place, whose in ((give_ref, others, 1 - core), (keep_ref, mine, core)):
         start = (2 * chip + whose) * rows
         live = start + lax.broadcasted_iota(jnp.int32, (rows, 1), 0) < len_ref[0]
@@ -337,28 +344,17 @@
         copy.wait()
 
 
-def rab_kernel(row_ref, rab_ref, *, total_len):
+def rab_kernel(rows_ref, rab_ref, *, total_len):
     heads, bands = rab_ref.shape
-    row = row_ref[...] / total_len
+    row = jnp.sum(rows_ref[...], axis=0)[:1] / total_len
     for head in range(heads):
         rab_ref[head : head + 1, :] = row[:, head * bands : (head + 1) * bands]
 
 
-def sum_over(value, axis, size, flip=1):
-    while flip < size:
-        value = value + lax.ppermute(value, axis, [(n, n ^ flip) for n in range(size)])
-        flip *= 2
-    return value
-
-
-def params(units, span, wide, **more):
+def params(**more):
     return dict(
         compiler_params=pltpu.CompilerParams(vmem_limit_bytes=VMEM_LIMIT),
-        cost_estimate=pl.CostEstimate(
-            flops=int(units * 8 * span * span * wide * 10),
-            bytes_accessed=int((units + 2) * 4 * span * wide),
-            transcendentals=0,
-        ),
+        cost_estimate=pl.CostEstimate(flops=1, bytes_accessed=1, transcendentals=0),
         **more,
     )
 
@@ -412,48 +408,66 @@
         in_specs=[SMEM, VMEM, VMEM],
         out_specs=(VMEM,) * 2,
         scratch_shapes=[cum],
-        **params(2, span, wide, name="attend_own"),
+        **params(name="attend_own"),
     )(rab_steps, own_kv, own_qd)
 
     acc_now, got[0] = lax.optimization_barrier((acc_now, got[0]))
     for n, one in enumerate(early):
         if got[n] is None:
             got[n] = send(got[one.payload], one.route)
-    ahead = send(got[late[0].payload], late[0].route)
-    acc_now, row = pl.pallas_call(
-        functools.partial(
-            middle_kernel, rounds=early, key_side=key_side, ends=ends, blocks_of=blocks_of, scale=scale
-        ),
-        out_shape=(acc, jax.ShapeDtypeStruct((1, 128), F32)),
-        in_specs=[SMEM] + [VMEM] * 4 + [ANY] * len(got),
-        out_specs=(VMEM,) * 2,
-        scratch_shapes=[
-            pltpu.VMEM((len(early), 2, span, wide), BF16),
-            pltpu.SemaphoreType.DMA((len(early),)),
-            pltpu.VMEM(rab.shape, F32),
+    def middle(state, done, upto, ends):
+        count = dp_size * seq_size if together else seq_size
+        second = rab if ends is None else jax.ShapeDtypeStruct((count, 8, 128), F32)
+        scratch = [
+            pltpu.VMEM((upto, 2, span, wide), BF16),
+            pltpu.SemaphoreType.DMA((upto,)),
             cum,
-            pltpu.SMEM((len(early), 2), jnp.int32),
-        ],
-        **params(len(early), span, wide, name="attend_middle"),
-    )(rab_steps, own_kv, own_qd, acc_now, rab_now, *got)
-
-    acc_now, ahead, *kept = lax.optimization_barrier((acc_now, ahead, *[got[one.payload] for one in late[1:]]))
-    tail = [ahead] + [send(value, one.route) for value, one in zip(kept, late[1:])]
-    row = row + lax.ppermute(row, "seq", across_chip)
-    row = sum_over(row, "dp", dp_size)
-    row, tail = lax.optimization_barrier((row, tail))
-    row = row + lax.ppermute(row, "seq", [(n, n ^ 2) for n in range(seq_size)])
+            pltpu.SMEM((upto, 2), jnp.int32),
+        ]
+        return pl.pallas_call(
+            functools.partial(
+                middle_kernel,
+                rounds=early[:upto],
+                done=done,
+                key_side=key_side,
+                ends=ends,
+                blocks_of=blocks_of,
+                scale=scale,
+            ),
+            out_shape=(acc, second),
+            in_specs=[SMEM] + [VMEM] * 4 + [ANY] * upto,
+            out_specs=(VMEM,) * 2,
+            scratch_shapes=scratch if ends is None else scratch + [pltpu.VMEM(rab.shape, F32)],
+            **params(name="attend_next" if ends is None else "attend_middle"),
+        )(rab_steps, own_kv, own_qd, *state, *got[:upto])
+
+    together = dp_size * seq_size <= 64
+    tail = [send(got[late[0].payload], late[0].route)]
+    state = middle((acc_now, rab_now), 0, 1, None)
+    state, got[1:] = lax.optimization_barrier((state, got[1:]))
+    tail += [send(got[one.payload], one.route) for one in late[1:]]
+    acc_now, band = middle(state, 1, len(early), ends)
+    band, tail[0] = lax.optimization_barrier((band, tail[0]))
+    band = lax.all_to_all(band, ("dp", "seq") if together else "seq", 0, 0)
+    acc_now = pl.pallas_call(
+        functools.partial(late_kernel, rounds=late, blocks_of=blocks_of),
+        out_shape=acc,
+        in_specs=[SMEM] + [VMEM] * (3 + len(tail)),
+        out_specs=VMEM,
+        scratch_shapes=[cum],
+        **params(name="attend_late"),
+    )(rab_steps, own_kv, own_qd, acc_now, *tail)
+    acc_now, band = lax.optimization_barrier((acc_now, band))
+    if not together:
+        band = lax.psum(jnp.sum(band, axis=0, keepdims=True), "dp")
     half_out = jax.ShapeDtypeStruct((5, rows, wide), BF16)
     keep, give = pl.pallas_call(
-        functools.partial(last_kernel, rounds=late, blocks_of=blocks_of, scale=scale, inv_root=inv_root),
+        functools.partial(results_kernel, scale=scale, inv_root=inv_root),
         out_shape=(half_out, half_out),
-        in_specs=[SMEM, SMEM] + [VMEM] * (4 + len(tail)),
+        in_specs=[SMEM, VMEM, VMEM],
         out_specs=(VMEM,) * 2,
-        scratch_shapes=[pltpu.VMEM(acc.shape, F32), pltpu.VMEM(rab.shape, F32), cum],
-        **params(len(late), span, wide, name="attend_last"),
-    )(rab_steps, lengths, own_kv, own_qd, acc_now, gate, *tail)
-    row, give = lax.optimization_barrier((row, give))
-    row = sum_over(row, "seq", seq_size, 4)
+        **params(name="results"),
+    )(lengths, acc_now, gate)
     theirs = lax.ppermute(give, "seq", across_chip)
     out = jax.ShapeDtypeStruct(queries.shape, BF16)
     outs = pl.pallas_call(
@@ -462,16 +476,15 @@
         in_specs=[VMEM] * 2,
         out_specs=(HBM,) * 5,
         scratch_shapes=[pltpu.VMEM((5, rows, width), BF16), pltpu.SemaphoreType.DMA((5,))],
-        compiler_params=pltpu.CompilerParams(vmem_limit_bytes=VMEM_LIMIT),
-        name="assemble",
+        **params(name="assemble"),
     )(keep, theirs)
     rab_grad = pl.pallas_call(
         functools.partial(rab_kernel, total_len=total_len),
         out_shape=jax.ShapeDtypeStruct((heads, bands), F32),
         in_specs=[VMEM],
         out_specs=VMEM,
-        name="bias_grad",
-    )(row)
+        **params(name="bias_grad"),
+    )(band)
     return (*outs, rab_grad)
 
 

time: 48.3 us -> 43.9 us (0.909)
  waiting for transfers between devices: 17 us -> 13.2 us
  starting transfers between devices: 17.7 us -> 16.8 us
  Pallas kernels: 10.4 us -> 11.2 us
  other arithmetic: 0.53 us -> 0 us
    ppermute x5 -> x0, starting transfers between devices: 8.4 us -> none  [the longest x3 6.12 us: sum_over(): lax.ppermute(value, axis, [(n, n ^ flip) for n in range(size)])]
    ppermute x5 -> x0, waiting for transfers between devices: 6.78 us -> none  [the longest x3 5.66 us: sum_over(): lax.ppermute(value, axis, [(n, n ^ flip) for n in range(size)])]
    all_to_all x0 -> x1, waiting for transfers between devices: none -> 5.03 us  [body(): band = lax.all_to_all(band, ('dp', 'seq') if together else 'seq', 0, 0)]
    ppermute x5, starting transfers between devices: 8.67 us -> 12.7 us  [send(): return lax.ppermute(value, 'seq', pairs)]
    all_to_all x0 -> x1, starting transfers between devices: none -> 3.26 us  [body(): band = lax.all_to_all(band, ('dp', 'seq') if together else 'seq', 0, 0)]
    ppermute x5, waiting for transfers between devices: 8.66 us -> 5.99 us  [send(): return lax.ppermute(value, 'seq', pairs)]
    pallas_call x2 -> x4, Pallas kernels: 4.03 us -> 5.39 us  [the longest x2 3.15 us: middle(): pl.pallas_call(functools.partial(middle_kernel, rounds=early[:upto], done...]
    ppermute x1, waiting for transfers between devices: 0.01 us -> 0.63 us  [body(): theirs = lax.ppermute(give, 'seq', across_chip)]
  transfers between devices with their start and end apart: 12 -> 8, of which waited for: 9 -> 6; matrix products, arithmetic and copies ran while one was open for 1% -> 0% of each run, Pallas kernels for 15% -> 18%
where the time goes in v3:
time: 43.9 us; the launch traced here: 43.6 us
  starting transfers between devices  16.8 us (38%)
  waiting for transfers between devices  13.2 us (30%)
  Pallas kernels  11.2 us (26%)
  between operations  1.4 us (3%)
  local copies, waits for them, and re-layouts  1 us (2%)
    ppermute x5, starting transfers between devices, send(): return lax.ppermute(value, 'seq', pairs)  12.7 us
    ppermute x5, waiting for transfers between devices, send(): return lax.ppermute(value, 'seq', pairs)  5.99 us
    all_to_all x1, waiting for transfers between devices, body(): band = lax.all_to_all(band, ('dp', 'seq') if together else 'seq', 0, 0)  5.03 us
    all_to_all x1, starting transfers between devices, body(): band = lax.all_to_all(band, ('dp', 'seq') if together else 'seq', 0, 0)  3.26 us
    pallas_call x2, Pallas kernels, middle(): pl.pallas_call(functools.partial(middle_kernel, rounds=early[:upto], done...  3.15 us
    pallas_call x1, Pallas kernels, body(): pl.pallas_call(prep_kernel, out_shape=(packed, packed), in_specs=[SMEM] +...  2.19 us
    pallas_call x1, Pallas kernels, body(): pl.pallas_call(functools.partial(late_kernel, rounds=late, blocks_of=bloc...  2.11 us
    pallas_call x1, Pallas kernels, body(): pl.pallas_call(functools.partial(own_kernel, blocks_of=blocks_of), out_sh...  1.87 us
  transfers between devices with their start and end apart: 8, of which 6 were waited for; matrix products, arithmetic and copies ran while one was open for 0% of the time, Pallas kernels for 18%

profile of v3, /device:TPU:0, one launch (start us, length us, event | category | flops | bytes accessed | tf_op | source)
XLA Modules:
  0.0 43.6 jit_solution(15342754686978211555)
XLA Ops:
  1.3 2.2 %prep.1 = (bf16[6,128,256]{2,1,0:T(8,128)(2,1)}, bf16[6,128,256]{2,1,0:T(8,128)(2,1)}) custom-call(s32[1]{0:T(128)S(6)} %copy.13.len_ref, bf16[1,128,512]{2,1,0:T(8,128)(2,1)} %k_ref.1, bf16[1,128,512]{2,1,0:T(8,128)(2,1)} %v_ref.1, bf16[1,128,512]{2,1,0:T(8,128)(2,1)} %q_ref.1, bf16[1,128,512]{2,1,0:T(8,128)(2,1)} %u_ref.1, bf16[1,128,512]{2,1,0:T(8,128)(2,1)} %og_ref.1), custom_call_target="tpu_custom_call" | custom-call | tf_op jit(solution)/shard_map/prep/pallas_call | solution.py:379
  3.5 0.5 %collective-permute-start = (bf16[6,128,256]{2,1,0:T(8,128)(2,1)}, bf16[6,128,256]{2,1,0:T(8,128)(2,1)S(1)}, u32[]{:S(2)}, u32[]{:S(2)}) collective-permute-start(bf16[6,128,256]{2,1,0:T(8,128)(2,1)} %get-tuple-element.37), channel_id=1, source_target_pairs={{0,1},{1,0},{2,3},{3,2},{4,5},{5,4},{6,7},{7,6},{8,9},{9,8},{10,11... | collective-permute-start | bytes 1179656 | tf_op jit(solution)/shard_map/ppermute | solution.py:396
  4.0 1.6 %collective-permute-done.near_ref = bf16[6,128,256]{2,1,0:T(8,128)(2,1)S(1)} collective-permute-done((bf16[6,128,256]{2,1,0:T(8,128)(2,1)}, bf16[6,128,256]{2,1,0:T(8,128)(2,1)S(1)}, u32[]{:S(2)}, u32[]{:S(2)}) %collective-permute-start) | collective-permute-done | bytes 393248 | tf_op jit(solution)/shard_map/ppermute | solution.py:396
  5.6 0.0 copy-start
  5.6 1.0 %copy-done = bf16[6,128,256]{2,1,0:T(8,128)(2,1)S(1)} copy-done((bf16[6,128,256]{2,1,0:T(8,128)(2,1)S(1)}, bf16[6,128,256]{2,1,0:T(8,128)(2,1)}, u32[]{:S(2)}) %copy-start) | copy-done | bytes 393240
  6.6 0.1 build.1
  6.7 4.0 %collective-permute-start.1 = (bf16[2,256,256]{2,1,0:T(8,128)(2,1)S(1)}, bf16[2,256,256]{2,1,0:T(8,128)(2,1)S(1)}, u32[]{:S(2)}, u32[]{:S(2)}) collective-permute-start(bf16[2,256,256]{2,1,0:T(8,128)(2,1)S(1)} %get-tuple-element.41), channel_id=1, source_target_pairs={{0,4},{1,5},{6,2},{7,3},{2,0},{3,1},{4,6},{5,7},{8,12},{9,13},{14,... | collective-permute-start | bytes 786440 | tf_op jit(solution)/shard_map/ppermute | solution.py:375
  10.7 0.0 copy-start.1
  10.7 0.8 %collective-permute-start.2 = (bf16[2,256,256]{2,1,0:T(8,128)(2,1)S(1)}, bf16[2,256,256]{2,1,0:T(8,128)(2,1)S(1)}, u32[]{:S(2)}, u32[]{:S(2)}) collective-permute-start(bf16[2,256,256]{2,1,0:T(8,128)(2,1)S(1)} %get-tuple-element.47), channel_id=1, source_target_pairs={{2,4},{3,5},{4,2},{5,3},{10,12},{11,13},{12,10},{13,11},{18,20},{1... | collective-permute-start | bytes 786440 | tf_op jit(solution)/shard_map/ppermute | solution.py:375
  11.5 5.3 %collective-permute-start.3 = (bf16[2,256,256]{2,1,0:T(8,128)(2,1)S(1)}, bf16[2,256,256]{2,1,0:T(8,128)(2,1)S(1)}, u32[]{:S(2)}, u32[]{:S(2)}) collective-permute-start(bf16[2,256,256]{2,1,0:T(8,128)(2,1)S(1)} %get-tuple-element.47), channel_id=1, source_target_pairs={{0,2},{1,3},{6,4},{7,5},{8,10},{9,11},{14,12},{15,13},{16,18},{17,... | collective-permute-start | bytes 786440 | tf_op jit(solution)/shard_map/ppermute | solution.py:375
  16.8 0.0 copy-done.1
  16.8 1.9 %attend_own.1 = (f32[2,2,256,256]{3,2,1,0:T(8,128)S(1)}, f32[2,2,17,8,128]{4,3,2,1,0:T(8,128)S(1)}) custom-call(f32[4,16]{1,0:T(4,128)S(1)} %copy-done.1, bf16[2,256,256]{2,1,0:T(8,128)(2,1)S(1)} %get-tuple-element.38.kv_ref.refs_1_, bf16[2,256,256]{2,1,0:T(8,128)(2,1)S(1)} %get-tuple-element.39.qd_ref.refs_2_), custom_call_target="tpu_custom_call" | custom-call | flops 1 | bytes 1 | tf_op jit(solution)/shard_map/attend_own/pallas_call | solution.py:405
  18.7 0.0 collective-permute-done.1.refs_5_
  18.7 1.3 %collective-permute-start.4 = (bf16[2,256,256]{2,1,0:T(8,128)(2,1)S(1)}, bf16[2,256,256]{2,1,0:T(8,128)(2,1)S(1)}, u32[]{:S(2)}, u32[]{:S(2)}) collective-permute-start(bf16[2,256,256]{2,1,0:T(8,128)(2,1)S(1)} %collective-permute-done.1.refs_5_), channel_id=1, source_target_pairs={{4,6},{5,7},{2,0},{3,1},{12,14},{13,15},{10,8},{11,9},{20,22},{21,... | collective-permute-start | bytes 786440 | tf_op jit(solution)/shard_map/ppermute | solution.py:375
  20.0 1.5 %attend_next.1 = (f32[2,2,256,256]{3,2,1,0:T(8,128)S(1)}, f32[2,2,17,8,128]{4,3,2,1,0:T(8,128)S(1)}) custom-call(f32[4,16]{1,0:T(4,128)S(1)} %copy-done.1, bf16[2,256,256]{2,1,0:T(8,128)(2,1)S(1)} %get-tuple-element.38.kv_ref.refs_1_, bf16[2,256,256]{2,1,0:T(8,128)(2,1)S(1)} %get-tuple-element.39.qd_ref.refs_2_, ...), custom_call_target="tpu_custom_call" | custom-call | flops 1 | bytes 1 | tf_op jit(solution)/shard_map/attend_next/pallas_call | solution.py:427
  21.5 0.0 collective-permute-done.2.refs_6_
  21.5 0.7 %collective-permute-done.3.refs_7_ = bf16[2,256,256]{2,1,0:T(8,128)(2,1)S(1)} collective-permute-done((bf16[2,256,256]{2,1,0:T(8,128)(2,1)S(1)}, bf16[2,256,256]{2,1,0:T(8,128)(2,1)S(1)}, u32[]{:S(2)}, u32[]{:S(2)}) %collective-permute-start.3) | collective-permute-done | bytes 262176 | tf_op jit(solution)/shard_map/ppermute | solution.py:375
  22.2 1.3 %collective-permute-start.5 = (bf16[2,256,256]{2,1,0:T(8,128)(2,1)S(1)}, bf16[2,256,256]{2,1,0:T(8,128)(2,1)S(1)}, u32[]{:S(2)}, u32[]{:S(2)}) collective-permute-start(bf16[2,256,256]{2,1,0:T(8,128)(2,1)S(1)} %collective-permute-done.2.refs_6_), channel_id=1, source_target_pairs={{4,6},{5,7},{2,0},{3,1},{12,14},{13,15},{10,8},{11,9},{20,22},{21,... | collective-permute-start | bytes 786440 | tf_op jit(solution)/shard_map/ppermute | solution.py:375
  23.5 1.6 %attend_middle.1 = (f32[2,2,256,256]{3,2,1,0:T(8,128)S(1)}, f32[32,8,128]{2,1,0:T(8,128)}) custom-call(f32[4,16]{1,0:T(4,128)S(1)} %copy-done.1, bf16[2,256,256]{2,1,0:T(8,128)(2,1)S(1)} %get-tuple-element.38.kv_ref.refs_1_, bf16[2,256,256]{2,1,0:T(8,128)(2,1)S(1)} %get-tuple-element.39.qd_ref.refs_2_, f32[2,2,256,256]{3,2,1,0:T(8,128)S(1)} %get-tuple-element.48.refs_3_, ...), custom_call_target="tpu_custom_call" | custom-call | flops 1 | bytes 1 | tf_op jit(solution)/shard_map/attend_middle/pallas_call | solution.py:427
  25.1 4.3 %collective-permute-done.4.refs_0_ = bf16[2,256,256]{2,1,0:T(8,128)(2,1)S(1)} collective-permute-done((bf16[2,256,256]{2,1,0:T(8,128)(2,1)S(1)}, bf16[2,256,256]{2,1,0:T(8,128)(2,1)S(1)}, u32[]{:S(2)}, u32[]{:S(2)}) %collective-permute-start.4) | collective-permute-done | bytes 262176 | tf_op jit(solution)/shard_map/ppermute | solution.py:375
  29.4 3.3 %all-to-all-start = ((f32[32,8,128]{2,1,0:T(8,128)}), f32[32,8,128]{2,1,0:T(8,128)S(1)}, u32[]{:S(2)}, u32[]{:S(2)}) async-start(f32[32,8,128]{2,1,0:T(8,128)} %get-tuple-element.55), calls=%async_computation | async-start | bytes 262144 | tf_op jit(solution)/shard_map/all_to_all | solution.py:451
  32.7 1.0 %collective-permute-done.5.refs_1_ = bf16[2,256,256]{2,1,0:T(8,128)(2,1)S(1)} collective-permute-done((bf16[2,256,256]{2,1,0:T(8,128)(2,1)S(1)}, bf16[2,256,256]{2,1,0:T(8,128)(2,1)S(1)}, u32[]{:S(2)}, u32[]{:S(2)}) %collective-permute-start.5) | collective-permute-done | bytes 262176 | tf_op jit(solution)/shard_map/ppermute | solution.py:375
  33.7 2.1 %attend_late.1.acc = f32[2,2,256,256]{3,2,1,0:T(8,128)S(1)} custom-call(f32[4,16]{1,0:T(4,128)S(1)} %copy-done.1, bf16[2,256,256]{2,1,0:T(8,128)(2,1)S(1)} %get-tuple-element.38.kv_ref.refs_1_, bf16[2,256,256]{2,1,0:T(8,128)(2,1)S(1)} %get-tuple-element.39.qd_ref.refs_2_, f32[2,2,256,256]{3,2,1,0:T(8,128)S(1)} %get-tuple-element.52.acc_in, ...), custom_call_target="tpu_custom_call" | custom-call | flops 1 | bytes 1 | tf_op jit(solution)/shard_map/attend_late/pallas_call | solution.py:452
  35.8 5.0 %all-to-all-done.rows_ref = f32[32,8,128]{2,1,0:T(8,128)S(1)} async-done(((f32[32,8,128]{2,1,0:T(8,128)}), f32[32,8,128]{2,1,0:T(8,128)S(1)}, u32[]{:S(2)}, u32[]{:S(2)}) %all-to-all-start) | async-done | bytes 131104 | tf_op jit(solution)/shard_map/all_to_all | solution.py:451
  40.8 0.1 results.1
  41.0 0.4 collective-permute-start.6
  41.4 0.7 %bias_grad.1 = f32[4,16]{1,0:T(4,128)} custom-call(f32[32,8,128]{2,1,0:T(8,128)S(1)} %all-to-all-done.rows_ref), custom_call_target="tpu_custom_call" | custom-call | flops 1 | bytes 1 | tf_op jit(solution)/shard_map/bias_grad/pallas_call | solution.py:481
  42.0 0.6 %collective-permute-done.6.got_ref = bf16[5,128,256]{2,1,0:T(8,128)(2,1)S(1)} collective-permute-done((bf16[5,128,256]{2,1,0:T(8,128)(2,1)S(1)}, bf16[5,128,256]{2,1,0:T(8,128)(2,1)S(1)}, u32[]{:S(2)}, u32[]{:S(2)}) %collective-permute-start.6) | collective-permute-done | bytes 327712 | tf_op jit(solution)/shard_map/ppermute | solution.py:471
  42.7 0.9 %assemble.1 = (bf16[1,128,512]{2,1,0:T(8,128)(2,1)}, bf16[1,128,512]{2,1,0:T(8,128)(2,1)}, bf16[1,128,512]{2,1,0:T(8,128)(2,1)}, bf16[1,128,512]{2,1,0:T(8,128)(2,1)}, bf16[1,128,512]{2,1,0:T(8,128)(2,1)}) custom-call(bf16[5,128,256]{2,1,0:T(8,128)(2,1)S(1)} %get-tuple-element.58.keep_ref, bf16[5,128,256]{2,1,0:T(8,128)(2,1)S(1)} %collective-permute-done.6.got_ref), custom_call_target="tpu_custom_call" | custom-call | flops 1 | bytes 1 | tf_op jit(solution)/shard_map/assemble/pallas_call | solution.py:473
Async XLA Ops:
  3.5 2.1 %collective-permute-start = (bf16[6,128,256]{2,1,0:T(8,128)(2,1)}, bf16[6,128,256]{2,1,0:T(8,128)(2,1)S(1)}, u32[]{:S(2)}, u32[]{:S(2)}) collective-permute-start(bf16[6,128,256]{2,1,0:T(8,128)(2,1)} %get-tuple-element.37), channel_id=1, source_target_pairs={{0,1},{1,0},{2,3},{3,2},{4,5},{5,4},{6,7},{7,6},{8,9},{9,8},{10,11... | collective-permute-start | bytes 1179656 | tf_op jit(solution)/shard_map/ppermute | solution.py:396
  5.6 1.0 %copy-start = (bf16[6,128,256]{2,1,0:T(8,128)(2,1)S(1)}, bf16[6,128,256]{2,1,0:T(8,128)(2,1)}, u32[]{:S(2)}) copy-start(bf16[6,128,256]{2,1,0:T(8,128)(2,1)} %get-tuple-element.36.same_ref) | copy-start | bytes 1179652
  6.7 12.0 %collective-permute-start.1 = (bf16[2,256,256]{2,1,0:T(8,128)(2,1)S(1)}, bf16[2,256,256]{2,1,0:T(8,128)(2,1)S(1)}, u32[]{:S(2)}, u32[]{:S(2)}) collective-permute-start(bf16[2,256,256]{2,1,0:T(8,128)(2,1)S(1)} %get-tuple-element.41), channel_id=1, source_target_pairs={{0,4},{1,5},{6,2},{7,3},{2,0},{3,1},{4,6},{5,7},{8,12},{9,13},{14,... | collective-permute-start | bytes 786440 | tf_op jit(solution)/shard_map/ppermute | solution.py:375
  10.7 6.1 %copy-start.1 = (f32[4,16]{1,0:T(4,128)S(1)}, f32[4,16]{1,0:T(4,128)}, u32[]{:S(2)}) copy-start(f32[4,16]{1,0:T(4,128)} %steps_ref.3) | copy-start | bytes 772
  10.7 10.8 %collective-permute-start.2 = (bf16[2,256,256]{2,1,0:T(8,128)(2,1)S(1)}, bf16[2,256,256]{2,1,0:T(8,128)(2,1)S(1)}, u32[]{:S(2)}, u32[]{:S(2)}) collective-permute-start(bf16[2,256,256]{2,1,0:T(8,128)(2,1)S(1)} %get-tuple-element.47), channel_id=1, source_target_pairs={{2,4},{3,5},{4,2},{5,3},{10,12},{11,13},{12,10},{13,11},{18,20},{1... | collective-permute-start | bytes 786440 | tf_op jit(solution)/shard_map/ppermute | solution.py:375
  11.5 10.7 %collective-permute-start.3 = (bf16[2,256,256]{2,1,0:T(8,128)(2,1)S(1)}, bf16[2,256,256]{2,1,0:T(8,128)(2,1)S(1)}, u32[]{:S(2)}, u32[]{:S(2)}) collective-permute-start(bf16[2,256,256]{2,1,0:T(8,128)(2,1)S(1)} %get-tuple-element.47), channel_id=1, source_target_pairs={{0,2},{1,3},{6,4},{7,5},{8,10},{9,11},{14,12},{15,13},{16,18},{17,... | collective-permute-start | bytes 786440 | tf_op jit(solution)/shard_map/ppermute | solution.py:375
  18.7 10.7 %collective-permute-start.4 = (bf16[2,256,256]{2,1,0:T(8,128)(2,1)S(1)}, bf16[2,256,256]{2,1,0:T(8,128)(2,1)S(1)}, u32[]{:S(2)}, u32[]{:S(2)}) collective-permute-start(bf16[2,256,256]{2,1,0:T(8,128)(2,1)S(1)} %collective-permute-done.1.refs_5_), channel_id=1, source_target_pairs={{4,6},{5,7},{2,0},{3,1},{12,14},{13,15},{10,8},{11,9},{20,22},{21,... | collective-permute-start | bytes 786440 | tf_op jit(solution)/shard_map/ppermute | solution.py:375
  22.2 11.5 %collective-permute-start.5 = (bf16[2,256,256]{2,1,0:T(8,128)(2,1)S(1)}, bf16[2,256,256]{2,1,0:T(8,128)(2,1)S(1)}, u32[]{:S(2)}, u32[]{:S(2)}) collective-permute-start(bf16[2,256,256]{2,1,0:T(8,128)(2,1)S(1)} %collective-permute-done.2.refs_6_), channel_id=1, source_target_pairs={{4,6},{5,7},{2,0},{3,1},{12,14},{13,15},{10,8},{11,9},{20,22},{21,... | collective-permute-start | bytes 786440 | tf_op jit(solution)/shard_map/ppermute | solution.py:375
  29.4 11.4 %all-to-all-start = ((f32[32,8,128]{2,1,0:T(8,128)}), f32[32,8,128]{2,1,0:T(8,128)S(1)}, u32[]{:S(2)}, u32[]{:S(2)}) async-start(f32[32,8,128]{2,1,0:T(8,128)} %get-tuple-element.55), calls=%async_computation | async-start | bytes 262144 | tf_op jit(solution)/shard_map/all_to_all | solution.py:451
  41.0 1.7 %collective-permute-start.6 = (bf16[5,128,256]{2,1,0:T(8,128)(2,1)S(1)}, bf16[5,128,256]{2,1,0:T(8,128)(2,1)S(1)}, u32[]{:S(2)}, u32[]{:S(2)}) collective-permute-start(bf16[5,128,256]{2,1,0:T(8,128)(2,1)S(1)} %get-tuple-element.59), channel_id=1, source_target_pairs={{0,1},{1,0},{2,3},{3,2},{4,5},{5,4},{6,7},{7,6},{8,9},{9,8},{10,11... | collective-permute-start | bytes 983048 | tf_op jit(solution)/shard_map/ppermute | solution.py:471

commit v4 on v3

--- a/solution.py
+++ b/solution.py
@@ -38,12 +38,12 @@
         return len(rounds) - 1
 
     if chips == 4:
-        across = add(early, "even", {0: 2, 3: 1, 1: 0, 2: 3})
         inner = add(early, "low", {1: 2, 2: 1})
         outer = add(early, "low", {0: 1, 3: 2})
+        across = add(early, "even", {0: 2, 3: 1, 1: 0, 2: 3})
+        add(late, inner, {2: 3, 1: 0})
         add(late, across, {2: 3, 1: 0})
-        add(late, inner, {2: 3, 1: 0})
-        return early, late, {across: (1,)}, {1: (across, outer, 0), 2: (outer, across, 1)}
+        return early, 2, late, {across: (1,)}, {1: (across, outer, 0), 2: (outer, across, 1)}
     far = add(early, "low", {n: n + half if n < half else n - half for n in range(chips)})
     for hops in range(1, half):
         up = add(early, "kv", {n: n + hops for n in range(chips - hops)})
@@ -52,7 +52,7 @@
     for hops in range(half, chips - 1):
         route = {n: n + 1 for n in range(hops, chips - 1)} | {n: n - 1 for n in range(1, chips - hops)}
         held = add(early if hops < chips - 2 else late, held, route)
-    return early, late, {}, {half - 1: (far, up, 0), half: (down, far, 1)}
+    return early, 1, late, {}, {half - 1: (far, up, 0), half: (down, far, 1)}
 
 
 def of_chip(table, chip):
@@ -395,7 +395,7 @@
         name="build",
     )(same, lax.ppermute(cross, "seq", across_chip))
 
-    early, late, key_side, ends = plan_rounds(chips)
+    early, split, late, key_side, ends = plan_rounds(chips)
     ready = {"kv": own_kv, "qd": own_qd, "low": low, "even": even}
     got = [send(ready[one.payload], one.route) if isinstance(one.payload, str) else None for one in early]
 
@@ -411,10 +411,11 @@
         **params(name="attend_own"),
     )(rab_steps, own_kv, own_qd)
 
-    acc_now, got[0] = lax.optimization_barrier((acc_now, got[0]))
+    acc_now, got[:split] = lax.optimization_barrier((acc_now, got[:split]))
     for n, one in enumerate(early):
         if got[n] is None:
             got[n] = send(got[one.payload], one.route)
+
     def middle(state, done, upto, ends):
         count = dp_size * seq_size if together else seq_size
         second = rab if ends is None else jax.ShapeDtypeStruct((count, 8, 128), F32)
@@ -442,12 +443,13 @@
         )(rab_steps, own_kv, own_qd, *state, *got[:upto])
 
     together = dp_size * seq_size <= 64
-    tail = [send(got[late[0].payload], late[0].route)]
-    state = middle((acc_now, rab_now), 0, 1, None)
-    state, got[1:] = lax.optimization_barrier((state, got[1:]))
-    tail += [send(got[one.payload], one.route) for one in late[1:]]
-    acc_now, band = middle(state, 1, len(early), ends)
-    band, tail[0] = lax.optimization_barrier((band, tail[0]))
+    tail = [send(got[one.payload], one.route) for one in late if one.payload < split]
+    ahead = len(tail)
+    state = middle((acc_now, rab_now), 0, split, None)
+    state, got[split:] = lax.optimization_barrier((state, got[split:]))
+    tail += [send(got[one.payload], one.route) for one in late if one.payload >= split]
+    acc_now, band = middle(state, split, len(early), ends)
+    band, tail[:ahead] = lax.optimization_barrier((band, tail[:ahead]))
     band = lax.all_to_all(band, ("dp", "seq") if together else "seq", 0, 0)
     acc_now = pl.pallas_call(
         functools.partial(late_kernel, rounds=late, blocks_of=blocks_of),

time: 43.9 us -> 51.2 us (1.17)
  waiting for transfers between devices: 13.2 us -> 20.9 us
    ppermute x5, waiting for transfers between devices: 5.99 us -> 12.7 us  [send(): return lax.ppermute(value, 'seq', pairs)]
    ppermute x5, starting transfers between devices: 12.7 us -> 10.2 us  [send(): return lax.ppermute(value, 'seq', pairs)]
    all_to_all x1, starting transfers between devices: 3.26 us -> 5.29 us  [body(): band = lax.all_to_all(band, ('dp', 'seq') if together else 'seq', 0, 0)]
    all_to_all x1, waiting for transfers between devices: 5.03 us -> 6.04 us  [body(): band = lax.all_to_all(band, ('dp', 'seq') if together else 'seq', 0, 0)]
  transfers between devices with their start and end apart: 8 -> 8, of which waited for: 6 -> 6; matrix products, arithmetic and copies ran while one was open for 0% -> 0% of each run, Pallas kernels for 18% -> 15%
where the time goes in v4:
time: 51.2 us; the launch traced here: 50.9 us
  waiting for transfers between devices  20.9 us (41%)
  starting transfers between devices  16.4 us (32%)
  Pallas kernels  11.2 us (22%)
  between operations  1.39 us (3%)
  local copies, waits for them, and re-layouts  1 us (2%)
    ppermute x5, waiting for transfers between devices, send(): return lax.ppermute(value, 'seq', pairs)  12.7 us
    ppermute x5, starting transfers between devices, send(): return lax.ppermute(value, 'seq', pairs)  10.2 us
    all_to_all x1, waiting for transfers between devices, body(): band = lax.all_to_all(band, ('dp', 'seq') if together else 'seq', 0, 0)  6.04 us
    all_to_all x1, starting transfers between devices, body(): band = lax.all_to_all(band, ('dp', 'seq') if together else 'seq', 0, 0)  5.29 us
    pallas_call x2, Pallas kernels, middle(): pl.pallas_call(functools.partial(middle_kernel, rounds=early[:upto], done...  3.17 us
    pallas_call x1, Pallas kernels, body(): pl.pallas_call(prep_kernel, out_shape=(packed, packed), in_specs=[SMEM] +...  2.19 us
    pallas_call x1, Pallas kernels, body(): pl.pallas_call(functools.partial(late_kernel, rounds=late, blocks_of=bloc...  2.12 us
    pallas_call x1, Pallas kernels, body(): pl.pallas_call(functools.partial(own_kernel, blocks_of=blocks_of), out_sh...  1.86 us
  transfers between devices with their start and end apart: 8, of which 6 were waited for; matrix products, arithmetic and copies ran while one was open for 0% of the time, Pallas kernels for 15%

profile of v4, /device:TPU:0, one launch (start us, length us, event | category | flops | bytes accessed | tf_op | source)
XLA Modules:
  0.0 50.9 jit_solution(9536239437260206331)
XLA Ops:
  1.3 2.2 %prep.1 = (bf16[6,128,256]{2,1,0:T(8,128)(2,1)}, bf16[6,128,256]{2,1,0:T(8,128)(2,1)}) custom-call(s32[1]{0:T(128)S(6)} %copy.13.len_ref, bf16[1,128,512]{2,1,0:T(8,128)(2,1)} %k_ref.1, bf16[1,128,512]{2,1,0:T(8,128)(2,1)} %v_ref.1, bf16[1,128,512]{2,1,0:T(8,128)(2,1)} %q_ref.1, bf16[1,128,512]{2,1,0:T(8,128)(2,1)} %u_ref.1, bf16[1,128,512]{2,1,0:T(8,128)(2,1)} %og_ref.1), custom_call_target="tpu_custom_call" | custom-call | tf_op jit(solution)/shard_map/prep/pallas_call | solution.py:379
  3.5 0.5 %collective-permute-start = (bf16[6,128,256]{2,1,0:T(8,128)(2,1)}, bf16[6,128,256]{2,1,0:T(8,128)(2,1)S(1)}, u32[]{:S(2)}, u32[]{:S(2)}) collective-permute-start(bf16[6,128,256]{2,1,0:T(8,128)(2,1)} %get-tuple-element.37), channel_id=1, source_target_pairs={{0,1},{1,0},{2,3},{3,2},{4,5},{5,4},{6,7},{7,6},{8,9},{9,8},{10,11... | collective-permute-start | bytes 1179656 | tf_op jit(solution)/shard_map/ppermute | solution.py:396
  4.0 1.6 %collective-permute-done.near_ref = bf16[6,128,256]{2,1,0:T(8,128)(2,1)S(1)} collective-permute-done((bf16[6,128,256]{2,1,0:T(8,128)(2,1)}, bf16[6,128,256]{2,1,0:T(8,128)(2,1)S(1)}, u32[]{:S(2)}, u32[]{:S(2)}) %collective-permute-start) | collective-permute-done | bytes 393248 | tf_op jit(solution)/shard_map/ppermute | solution.py:396
  5.6 0.0 copy-start
  5.6 1.0 %copy-done = bf16[6,128,256]{2,1,0:T(8,128)(2,1)S(1)} copy-done((bf16[6,128,256]{2,1,0:T(8,128)(2,1)S(1)}, bf16[6,128,256]{2,1,0:T(8,128)(2,1)}, u32[]{:S(2)}) %copy-start) | copy-done | bytes 393240
  6.6 0.1 build.1
  6.7 4.9 %collective-permute-start.2 = (bf16[2,256,256]{2,1,0:T(8,128)(2,1)S(1)}, bf16[2,256,256]{2,1,0:T(8,128)(2,1)S(1)}, u32[]{:S(2)}, u32[]{:S(2)}) collective-permute-start(bf16[2,256,256]{2,1,0:T(8,128)(2,1)S(1)} %get-tuple-element.41), channel_id=1, source_target_pairs={{0,2},{1,3},{6,4},{7,5},{8,10},{9,11},{14,12},{15,13},{16,18},{17,... | collective-permute-start | bytes 786440 | tf_op jit(solution)/shard_map/ppermute | solution.py:375
  11.5 0.7 %collective-permute-start.1 = (bf16[2,256,256]{2,1,0:T(8,128)(2,1)S(1)}, bf16[2,256,256]{2,1,0:T(8,128)(2,1)S(1)}, u32[]{:S(2)}, u32[]{:S(2)}) collective-permute-start(bf16[2,256,256]{2,1,0:T(8,128)(2,1)S(1)} %get-tuple-element.41), channel_id=1, source_target_pairs={{2,4},{3,5},{4,2},{5,3},{10,12},{11,13},{12,10},{13,11},{18,20},{1... | collective-permute-start | bytes 786440 | tf_op jit(solution)/shard_map/ppermute | solution.py:375
  12.2 0.0 copy-start.1
  12.2 2.1 %collective-permute-start.3 = (bf16[2,256,256]{2,1,0:T(8,128)(2,1)S(1)}, bf16[2,256,256]{2,1,0:T(8,128)(2,1)S(1)}, u32[]{:S(2)}, u32[]{:S(2)}) collective-permute-start(bf16[2,256,256]{2,1,0:T(8,128)(2,1)S(1)} %get-tuple-element.48), channel_id=1, source_target_pairs={{0,4},{1,5},{6,2},{7,3},{2,0},{3,1},{4,6},{5,7},{8,12},{9,13},{14,... | collective-permute-start | bytes 786440 | tf_op jit(solution)/shard_map/ppermute | solution.py:375
  14.4 0.0 copy-done.1
  14.4 1.9 %attend_own.1 = (f32[2,2,256,256]{3,2,1,0:T(8,128)S(1)}, f32[2,2,17,8,128]{4,3,2,1,0:T(8,128)S(1)}) custom-call(f32[4,16]{1,0:T(4,128)S(1)} %copy-done.1, bf16[2,256,256]{2,1,0:T(8,128)(2,1)S(1)} %get-tuple-element.38.kv_ref.refs_1_, bf16[2,256,256]{2,1,0:T(8,128)(2,1)S(1)} %get-tuple-element.39.qd_ref.refs_2_), custom_call_target="tpu_custom_call" | custom-call | flops 1 | bytes 1 | tf_op jit(solution)/shard_map/attend_own/pallas_call | solution.py:405
  16.2 1.9 %collective-permute-done.2.refs_6_ = bf16[2,256,256]{2,1,0:T(8,128)(2,1)S(1)} collective-permute-done((bf16[2,256,256]{2,1,0:T(8,128)(2,1)S(1)}, bf16[2,256,256]{2,1,0:T(8,128)(2,1)S(1)}, u32[]{:S(2)}, u32[]{:S(2)}) %collective-permute-start.2) | collective-permute-done | bytes 262176 | tf_op jit(solution)/shard_map/ppermute | solution.py:375
  18.2 0.0 collective-permute-done.1.refs_5_
  18.2 1.3 %collective-permute-start.4 = (bf16[2,256,256]{2,1,0:T(8,128)(2,1)S(1)}, bf16[2,256,256]{2,1,0:T(8,128)(2,1)S(1)}, u32[]{:S(2)}, u32[]{:S(2)}) collective-permute-start(bf16[2,256,256]{2,1,0:T(8,128)(2,1)S(1)} %collective-permute-done.1.refs_5_), channel_id=1, source_target_pairs={{4,6},{5,7},{2,0},{3,1},{12,14},{13,15},{10,8},{11,9},{20,22},{21,... | collective-permute-start | bytes 786440 | tf_op jit(solution)/shard_map/ppermute | solution.py:375
  19.5 0.8 %attend_next.1 = (f32[2,2,256,256]{3,2,1,0:T(8,128)S(1)}, f32[2,2,17,8,128]{4,3,2,1,0:T(8,128)S(1)}) custom-call(f32[4,16]{1,0:T(4,128)S(1)} %copy-done.1, bf16[2,256,256]{2,1,0:T(8,128)(2,1)S(1)} %get-tuple-element.38.kv_ref.refs_1_, bf16[2,256,256]{2,1,0:T(8,128)(2,1)S(1)} %get-tuple-element.39.qd_ref.refs_2_, ...), custom_call_target="tpu_custom_call" | custom-call | flops 1 | bytes 1 | tf_op jit(solution)/shard_map/attend_next/pallas_call | solution.py:428
  20.2 2.8 %collective-permute-done.3.refs_7_ = bf16[2,256,256]{2,1,0:T(8,128)(2,1)S(1)} collective-permute-done((bf16[2,256,256]{2,1,0:T(8,128)(2,1)S(1)}, bf16[2,256,256]{2,1,0:T(8,128)(2,1)S(1)}, u32[]{:S(2)}, u32[]{:S(2)}) %collective-permute-start.3) | collective-permute-done | bytes 262176 | tf_op jit(solution)/shard_map/ppermute | solution.py:375
  23.0 1.3 %collective-permute-start.5 = (bf16[2,256,256]{2,1,0:T(8,128)(2,1)S(1)}, bf16[2,256,256]{2,1,0:T(8,128)(2,1)S(1)}, u32[]{:S(2)}, u32[]{:S(2)}) collective-permute-start(bf16[2,256,256]{2,1,0:T(8,128)(2,1)S(1)} %collective-permute-done.3.refs_7_), channel_id=1, source_target_pairs={{4,6},{5,7},{2,0},{3,1},{12,14},{13,15},{10,8},{11,9},{20,22},{21,... | collective-permute-start | bytes 786440 | tf_op jit(solution)/shard_map/ppermute | solution.py:375
  24.3 2.4 %attend_middle.1 = (f32[2,2,256,256]{3,2,1,0:T(8,128)S(1)}, f32[32,8,128]{2,1,0:T(8,128)}) custom-call(f32[4,16]{1,0:T(4,128)S(1)} %copy-done.1, bf16[2,256,256]{2,1,0:T(8,128)(2,1)S(1)} %get-tuple-element.38.kv_ref.refs_1_, bf16[2,256,256]{2,1,0:T(8,128)(2,1)S(1)} %get-tuple-element.39.qd_ref.refs_2_, f32[2,2,256,256]{3,2,1,0:T(8,128)S(1)} %get-tuple-element.49.refs_3_, ...), custom_call_target="tpu_custom_call" | custom-call | flops 1 | bytes 1 | tf_op jit(solution)/shard_map/attend_middle/pallas_call | solution.py:428
  26.7 7.9 %collective-permute-done.4.refs_0_ = bf16[2,256,256]{2,1,0:T(8,128)(2,1)S(1)} collective-permute-done((bf16[2,256,256]{2,1,0:T(8,128)(2,1)S(1)}, bf16[2,256,256]{2,1,0:T(8,128)(2,1)S(1)}, u32[]{:S(2)}, u32[]{:S(2)}) %collective-permute-start.4) | collective-permute-done | bytes 262176 | tf_op jit(solution)/shard_map/ppermute | solution.py:375
  34.7 5.3 %all-to-all-start = ((f32[32,8,128]{2,1,0:T(8,128)}), f32[32,8,128]{2,1,0:T(8,128)S(1)}, u32[]{:S(2)}, u32[]{:S(2)}) async-start(f32[32,8,128]{2,1,0:T(8,128)} %get-tuple-element.55), calls=%async_computation | async-start | bytes 262144 | tf_op jit(solution)/shard_map/all_to_all | solution.py:453
  40.0 0.0 collective-permute-done.5.refs_1_
  40.0 2.1 %attend_late.1.acc = f32[2,2,256,256]{3,2,1,0:T(8,128)S(1)} custom-call(f32[4,16]{1,0:T(4,128)S(1)} %copy-done.1, bf16[2,256,256]{2,1,0:T(8,128)(2,1)S(1)} %get-tuple-element.38.kv_ref.refs_1_, bf16[2,256,256]{2,1,0:T(8,128)(2,1)S(1)} %get-tuple-element.39.qd_ref.refs_2_, f32[2,2,256,256]{3,2,1,0:T(8,128)S(1)} %get-tuple-element.52.acc_in, ...), custom_call_target="tpu_custom_call" | custom-call | flops 1 | bytes 1 | tf_op jit(solution)/shard_map/attend_late/pallas_call | solution.py:454
  42.1 6.0 %all-to-all-done.rows_ref = f32[32,8,128]{2,1,0:T(8,128)S(1)} async-done(((f32[32,8,128]{2,1,0:T(8,128)}), f32[32,8,128]{2,1,0:T(8,128)S(1)}, u32[]{:S(2)}, u32[]{:S(2)}) %all-to-all-start) | async-done | bytes 131104 | tf_op jit(solution)/shard_map/all_to_all | solution.py:453
  48.1 0.1 results.1
  48.3 0.4 collective-permute-start.6
  48.7 0.7 %bias_grad.1 = f32[4,16]{1,0:T(4,128)} custom-call(f32[32,8,128]{2,1,0:T(8,128)S(1)} %all-to-all-done.rows_ref), custom_call_target="tpu_custom_call" | custom-call | flops 1 | bytes 1 | tf_op jit(solution)/shard_map/bias_grad/pallas_call | solution.py:483
  49.3 0.6 %collective-permute-done.6.got_ref = bf16[5,128,256]{2,1,0:T(8,128)(2,1)S(1)} collective-permute-done((bf16[5,128,256]{2,1,0:T(8,128)(2,1)S(1)}, bf16[5,128,256]{2,1,0:T(8,128)(2,1)S(1)}, u32[]{:S(2)}, u32[]{:S(2)}) %collective-permute-start.6) | collective-permute-done | bytes 327712 | tf_op jit(solution)/shard_map/ppermute | solution.py:473
  50.0 0.9 %assemble.1 = (bf16[1,128,512]{2,1,0:T(8,128)(2,1)}, bf16[1,128,512]{2,1,0:T(8,128)(2,1)}, bf16[1,128,512]{2,1,0:T(8,128)(2,1)}, bf16[1,128,512]{2,1,0:T(8,128)(2,1)}, bf16[1,128,512]{2,1,0:T(8,128)(2,1)}) custom-call(bf16[5,128,256]{2,1,0:T(8,128)(2,1)S(1)} %get-tuple-element.58.keep_ref, bf16[5,128,256]{2,1,0:T(8,128)(2,1)S(1)} %collective-permute-done.6.got_ref), custom_call_target="tpu_custom_call" | custom-call | flops 1 | bytes 1 | tf_op jit(solution)/shard_map/assemble/pallas_call | solution.py:475
Async XLA Ops:
  3.5 2.1 %collective-permute-start = (bf16[6,128,256]{2,1,0:T(8,128)(2,1)}, bf16[6,128,256]{2,1,0:T(8,128)(2,1)S(1)}, u32[]{:S(2)}, u32[]{:S(2)}) collective-permute-start(bf16[6,128,256]{2,1,0:T(8,128)(2,1)} %get-tuple-element.37), channel_id=1, source_target_pairs={{0,1},{1,0},{2,3},{3,2},{4,5},{5,4},{6,7},{7,6},{8,9},{9,8},{10,11... | collective-permute-start | bytes 1179656 | tf_op jit(solution)/shard_map/ppermute | solution.py:396
  5.6 1.0 %copy-start = (bf16[6,128,256]{2,1,0:T(8,128)(2,1)S(1)}, bf16[6,128,256]{2,1,0:T(8,128)(2,1)}, u32[]{:S(2)}) copy-start(bf16[6,128,256]{2,1,0:T(8,128)(2,1)} %get-tuple-element.36.same_ref) | copy-start | bytes 1179652
  6.7 11.5 %collective-permute-start.2 = (bf16[2,256,256]{2,1,0:T(8,128)(2,1)S(1)}, bf16[2,256,256]{2,1,0:T(8,128)(2,1)S(1)}, u32[]{:S(2)}, u32[]{:S(2)}) collective-permute-start(bf16[2,256,256]{2,1,0:T(8,128)(2,1)S(1)} %get-tuple-element.41), channel_id=1, source_target_pairs={{0,2},{1,3},{6,4},{7,5},{8,10},{9,11},{14,12},{15,13},{16,18},{17,... | collective-permute-start | bytes 786440 | tf_op jit(solution)/shard_map/ppermute | solution.py:375
  11.5 6.6 %collective-permute-start.1 = (bf16[2,256,256]{2,1,0:T(8,128)(2,1)S(1)}, bf16[2,256,256]{2,1,0:T(8,128)(2,1)S(1)}, u32[]{:S(2)}, u32[]{:S(2)}) collective-permute-start(bf16[2,256,256]{2,1,0:T(8,128)(2,1)S(1)} %get-tuple-element.41), channel_id=1, source_target_pairs={{2,4},{3,5},{4,2},{5,3},{10,12},{11,13},{12,10},{13,11},{18,20},{1... | collective-permute-start | bytes 786440 | tf_op jit(solution)/shard_map/ppermute | solution.py:375
  12.2 2.1 %copy-start.1 = (f32[4,16]{1,0:T(4,128)S(1)}, f32[4,16]{1,0:T(4,128)}, u32[]{:S(2)}) copy-start(f32[4,16]{1,0:T(4,128)} %steps_ref.3) | copy-start | bytes 772
  12.2 10.8 %collective-permute-start.3 = (bf16[2,256,256]{2,1,0:T(8,128)(2,1)S(1)}, bf16[2,256,256]{2,1,0:T(8,128)(2,1)S(1)}, u32[]{:S(2)}, u32[]{:S(2)}) collective-permute-start(bf16[2,256,256]{2,1,0:T(8,128)(2,1)S(1)} %get-tuple-element.48), channel_id=1, source_target_pairs={{0,4},{1,5},{6,2},{7,3},{2,0},{3,1},{4,6},{5,7},{8,12},{9,13},{14,... | collective-permute-start | bytes 786440 | tf_op jit(solution)/shard_map/ppermute | solution.py:375
  18.2 16.5 %collective-permute-start.4 = (bf16[2,256,256]{2,1,0:T(8,128)(2,1)S(1)}, bf16[2,256,256]{2,1,0:T(8,128)(2,1)S(1)}, u32[]{:S(2)}, u32[]{:S(2)}) collective-permute-start(bf16[2,256,256]{2,1,0:T(8,128)(2,1)S(1)} %collective-permute-done.1.refs_5_), channel_id=1, source_target_pairs={{4,6},{5,7},{2,0},{3,1},{12,14},{13,15},{10,8},{11,9},{20,22},{21,... | collective-permute-start | bytes 786440 | tf_op jit(solution)/shard_map/ppermute | solution.py:375
  23.0 16.9 %collective-permute-start.5 = (bf16[2,256,256]{2,1,0:T(8,128)(2,1)S(1)}, bf16[2,256,256]{2,1,0:T(8,128)(2,1)S(1)}, u32[]{:S(2)}, u32[]{:S(2)}) collective-permute-start(bf16[2,256,256]{2,1,0:T(8,128)(2,1)S(1)} %collective-permute-done.3.refs_7_), channel_id=1, source_target_pairs={{4,6},{5,7},{2,0},{3,1},{12,14},{13,15},{10,8},{11,9},{20,22},{21,... | collective-permute-start | bytes 786440 | tf_op jit(solution)/shard_map/ppermute | solution.py:375
  34.7 13.5 %all-to-all-start = ((f32[32,8,128]{2,1,0:T(8,128)}), f32[32,8,128]{2,1,0:T(8,128)S(1)}, u32[]{:S(2)}, u32[]{:S(2)}) async-start(f32[32,8,128]{2,1,0:T(8,128)} %get-tuple-element.55), calls=%async_computation | async-start | bytes 262144 | tf_op jit(solution)/shard_map/all_to_all | solution.py:453
  48.3 1.7 %collective-permute-start.6 = (bf16[5,128,256]{2,1,0:T(8,128)(2,1)S(1)}, bf16[5,128,256]{2,1,0:T(8,128)(2,1)S(1)}, u32[]{:S(2)}, u32[]{:S(2)}) collective-permute-start(bf16[5,128,256]{2,1,0:T(8,128)(2,1)S(1)} %get-tuple-element.59), channel_id=1, source_target_pairs={{0,1},{1,0},{2,3},{3,2},{4,5},{5,4},{6,7},{7,6},{8,9},{9,8},{10,11... | collective-permute-start | bytes 983048 | tf_op jit(solution)/shard_map/ppermute | solution.py:473
